TPU v7x, 256 devices: a whole 4x4x8 slice. The times are simulated.
256 devices in a mesh: section: 16 (over y, x), dp: 16 (over z, core).
Axes of the slice: x: 4, y: 4, z: 8, core: 2. Of those that a mesh axis runs over, the one named last changes fastest.
Arguments:
- inputs: bfloat16 [8, 256, 2560], P(None, 'dp'), may hold values from -6 to 6
- cotangent: bfloat16 [8, 256, 2560], P(None, 'dp'), may hold values from -6 to 6
- weights: bfloat16 [16, 2560, 2560], P('section', 'dp'), may hold values from -0.0625 to 0.0625
- old_factor: float32 [16, 8, 640, 640], P('section', None, 'dp'), as said below
- plan: int32 [16, 3], replicated, may hold values from 0 to 15, as said below
- order: int32 [8], replicated, may hold values from 0 to 7, each once
Outputs:
- section_out: bfloat16 [16, 8, 256, 2560], P('section', None, 'dp')
- section_grad: bfloat16 [16, 8, 256, 2560], P('section', None, 'dp')
- inverse: float32 [16, 640, 640], P('section', 'dp')
Inputs may be any that keep to these rules, and one draw needn't show every extreme that they name: plan[s, 0] is a block of 0 to 7; plan[s, 1] is s or (s + 8) mod 16; plan[s, 2] is 1 to 8. `old_factor`: each block is symmetric with a positive diagonal that exceeds the sum of the absolute values of the rest of its row.
All inputs are finite; a program needn't handle non-finite values. Where the computation divides by a largest or mean magnitude, that divisor is 1e-20 or more.
Results may differ from a plain program's by a relative error of at most 0.023.
Values may be sent and summed in bfloat16 or wider, within the bound.
A program may use at most 64 MiB of HBM per device.

v0:
```python
import jax
import jax.numpy as jnp
from jax import lax
from jax.sharding import PartitionSpec as P

ITERS = 3


RETAIN = 0.6
DAMPING = 0.1


def from_behind(value, axis, steps):
    count = lax.axis_size(axis)
    initial, last = (max(0, -steps), min(count, count - steps))
    return lax.ppermute(value, axis, [(source, source + steps) for source in range(initial, last)])


def from_behind_2(value, axis, steps):
    count = lax.axis_size(axis)
    pairs = [(source, (source + steps) % count) for source in range(count)]
    return lax.ppermute(value, axis, pairs)


def for_sending(value):
    return jax.tree.map(lambda a: a.astype(jnp.bfloat16) if a.dtype == jnp.float32 else a, value)


def newton_schulz(matrix):
    order_size = matrix.shape[0]
    identity = jnp.eye(order_size, dtype=jnp.float32)
    row_bound = jnp.max(jnp.sum(jnp.abs(matrix), axis=1))
    approx = identity / row_bound
    for iteration in range(ITERS):
        product = jnp.dot(
            matrix, approx, precision=lax.Precision.HIGHEST, preferred_element_type=jnp.float32
        )
        approx = jnp.dot(
            approx,
            2.0 * identity - product,
            precision=lax.Precision.HIGHEST,
            preferred_element_type=jnp.float32,
        )
    return approx


def blank_like(matrix):
    return jnp.zeros_like(matrix)


def shards(inputs, cotangent, weights, old_factor, plan, order):
    sections = lax.axis_size("section")
    replicas = lax.axis_size("dp")
    my_section = lax.axis_index("section")
    replica = lax.axis_index("dp")
    micro_count, row_count, model_width = inputs.shape
    blocks = old_factor.shape[1]
    band_rows = old_factor.shape[2]
    order_size = old_factor.shape[3]
    tick_count = micro_count + sections - 1
    clocks = jnp.arange(tick_count, dtype=jnp.int32)
    full_weight = lax.all_gather(weights[0], "dp", axis=0, tiled=True)

    def forward_tick(state_in, moment):
        incoming, kept_in, kept_pre, kept_out = state_in
        position = moment - my_section
        active = jnp.logical_and(position >= 0, position < micro_count)
        safe_pos = jnp.clip(position, 0, micro_count - 1)
        fresh_input = lax.dynamic_index_in_dim(inputs, order[safe_pos], 0, keepdims=False)
        current = jnp.where(my_section == 0, fresh_input, incoming)

        def forward_compute(packed):
            current, kept_in, kept_pre, kept_out = packed
            preact = jnp.dot(current, full_weight, preferred_element_type=jnp.float32)
            output = (current.astype(jnp.float32) + jax.nn.silu(preact)).astype(jnp.bfloat16)
            kept_in = lax.dynamic_update_index_in_dim(kept_in, current, safe_pos, 0)
            kept_pre = lax.dynamic_update_index_in_dim(kept_pre, preact, safe_pos, 0)
            kept_out = lax.dynamic_update_index_in_dim(kept_out, output, safe_pos, 0)
            return (output, kept_in, kept_pre, kept_out)

        def forward_skipped(packed):
            current, kept_in, kept_pre, kept_out = packed
            return (jnp.zeros_like(current), kept_in, kept_pre, kept_out)

        output, kept_in, kept_pre, kept_out = lax.cond(
            active, forward_compute, forward_skipped, (current, kept_in, kept_pre, kept_out)
        )
        incoming = from_behind(output, "section", 1)
        return ((incoming, kept_in, kept_pre, kept_out), None)

    empty_acts = jnp.zeros((micro_count, row_count, model_width), jnp.bfloat16)
    empty_pre = jnp.zeros((micro_count, row_count, model_width), jnp.float32)
    start_in = jnp.zeros((row_count, model_width), jnp.bfloat16)
    forward_state, unused_fwd = lax.scan(
        forward_tick, (start_in, empty_acts, empty_pre, empty_acts), clocks
    )
    last_in, kept_in, kept_pre, kept_out = forward_state

    def backward_tick(state_in, moment):
        incoming, kept_delta, kept_grad = state_in
        position = moment - (sections - 1 - my_section)
        active = jnp.logical_and(position >= 0, position < micro_count)
        safe_pos = jnp.clip(position, 0, micro_count - 1)
        seed_grad = lax.dynamic_index_in_dim(cotangent, order[safe_pos], 0, keepdims=False)
        upstream = jnp.where(my_section == sections - 1, seed_grad, incoming)

        def backward_compute(packed):
            upstream, kept_delta, kept_grad = packed
            preact = lax.dynamic_index_in_dim(kept_pre, safe_pos, 0, keepdims=False)
            gating = jax.nn.sigmoid(preact)
            delta_now = (
                upstream.astype(jnp.float32) * gating * (1.0 + preact * (1.0 - gating))
            ).astype(jnp.bfloat16)
            backward = lax.dot_general(
                delta_now, full_weight, (((1,), (1,)), ((), ())), preferred_element_type=jnp.float32
            )
            gradient = (upstream.astype(jnp.float32) + backward).astype(jnp.bfloat16)
            kept_delta = lax.dynamic_update_index_in_dim(kept_delta, delta_now, safe_pos, 0)
            kept_grad = lax.dynamic_update_index_in_dim(kept_grad, gradient, safe_pos, 0)
            return (gradient, kept_delta, kept_grad)

        def backward_skipped(packed):
            upstream, kept_delta, kept_grad = packed
            return (jnp.zeros_like(upstream), kept_delta, kept_grad)

        gradient, kept_delta, kept_grad = lax.cond(
            active, backward_compute, backward_skipped, (upstream, kept_delta, kept_grad)
        )
        incoming = from_behind(gradient, "section", -1)
        return ((incoming, kept_delta, kept_grad), None)

    backward_state, unused_bwd = lax.scan(backward_tick, (start_in, empty_acts, empty_acts), clocks)
    last_grad, kept_delta, kept_grad = backward_state
    task_row = lax.dynamic_index_in_dim(plan, my_section, 0, keepdims=False)
    block_id = task_row[0]
    host_section = task_row[1]
    filled = task_row[2]
    partner_row = lax.dynamic_index_in_dim(
        plan, (my_section + sections // 2) % sections, 0, keepdims=False
    )
    shipped = host_section != my_section
    hosting = partner_row[1] == my_section
    half_count = blocks // 2
    offset = block_id % half_count * order_size
    flat_in = kept_in.reshape(micro_count * row_count, model_width)
    flat_delta = kept_delta.reshape(micro_count * row_count, model_width)
    features = jnp.where(
        block_id < half_count,
        lax.dynamic_slice_in_dim(flat_in, offset, order_size, 1),
        lax.dynamic_slice_in_dim(flat_delta, offset, order_size, 1),
    )
    positions = jnp.arange(micro_count * row_count, dtype=jnp.int32) // row_count
    masked = jnp.where((positions < filled)[:, None], features, jnp.zeros_like(features))
    partial_sum = lax.dot_general(
        masked, features, (((0,), (0,)), ((), ())), preferred_element_type=jnp.float32
    )
    scaled = partial_sum * ((1.0 - RETAIN) / (filled * row_count * replicas).astype(jnp.float32))
    old_rows = lax.dynamic_index_in_dim(old_factor[0], block_id, 0, keepdims=False)
    placed = lax.dynamic_update_slice(
        jnp.zeros((order_size, order_size), jnp.float32),
        RETAIN * old_rows,
        (replica * band_rows, jnp.int32(0)),
    )
    local_matrix = lax.psum((scaled + placed).astype(jnp.bfloat16), "dp").astype(
        jnp.float32
    ) + DAMPING * jnp.eye(order_size, dtype=jnp.float32)
    guest_matrix = from_behind_2(
        jnp.where(shipped, local_matrix, jnp.zeros_like(local_matrix)).astype(jnp.bfloat16),
        "section",
        sections // 2,
    ).astype(jnp.float32)
    own_inverse = lax.cond(shipped, blank_like, newton_schulz, local_matrix)
    guest_inverse = lax.cond(hosting, newton_schulz, blank_like, guest_matrix)
    guest_band = lax.dynamic_slice_in_dim(guest_inverse, replica * band_rows, band_rows, 0)
    returned = from_behind_2(for_sending(guest_band), "section", sections // 2).astype(
        guest_band.dtype
    )
    own_band = lax.dynamic_slice_in_dim(own_inverse, replica * band_rows, band_rows, 0)
    inverse_rows = jnp.where(shipped, returned, own_band)
    return (kept_out[None], kept_grad[None], inverse_rows[None])


def solution(mesh):
    return jax.shard_map(
        shards,
        mesh=mesh,
        in_specs=(
            P(None, "dp", None),
            P(None, "dp", None),
            P("section", "dp", None),
            P("section", None, "dp", None),
            P(),
            P(),
        ),
        out_specs=(
            P("section", None, "dp", None),
            P("section", None, "dp", None),
            P("section", "dp", None),
        ),
        check_vma=False,
    )
```

profile of v0, /device:TPU:8, one launch (start us, length us, event | category | flops | bytes accessed | tf_op | source)
XLA Modules:
  0.0 1158.2 jit_solution(3896441351374135439)
XLA Ops:
  14.6 76.3 %all-gather.3.cloned.1.call-done = bf16[1,2560,2560]{2,1,0:T(8,128)(2,1)} async-done(((bf16[1,160,2560]{2,1,0:T(8,128)(2,1)}), bf16[1,2560,2560]{2,1,0:T(8,128)(2,1)}) %all-gather.3.cloned.1.call-update) | async-done | bytes 13107216 | tf_op jit(solution)/shard_map/all_gather | solution.py:62
  91.1 358.0 %while.33 = (s32[]{:T(128)}, bf16[16,2560]{1,0:T(8,128)(2,1)S(1)}, bf16[8,16,2560]{2,1,0:T(8,128)(2,1)S(1)}, f32[8,16,2560]{2,1,0:T(8,128)S(1)}, bf16[8,16,2560]...) while((s32[]{:T(128)}, bf16[16,2560]{1,0:T(8,128)(2,1)S(1)}, ...), condition=%wide.region_3.4_spmd, body=%wide.region_0.3_spmd.sunk | while | flops 210042880 | bytes 14582198 | solution.py:94
  123.7 35.1 %collective-permute-done = bf16[16,2560]{1,0:T(8,128)(2,1)S(1)} collective-permute-done((bf16[16,2560]{1,0:T(8,128)(2,1)S(1)}, bf16[16,2560]{1,0:T(8,128)(2,1)S(1)}, u32[]{:S(2)}, u32[]{:S(2)}) %collective-permute-start) | collective-permute-done | bytes 81952 | tf_op jit(solution)/shard_map/while/body/eval_jaxpr/ppermute | solution.py:16
  160.0 10.2 conditional.8
  388.7 12.1 %collective-permute-start = (bf16[16,2560]{1,0:T(8,128)(2,1)S(1)}, bf16[16,2560]{1,0:T(8,128)(2,1)S(1)}, u32[]{:S(2)}, u32[]{:S(2)}) collective-permute-start(bf16[16,2560]{1,0:T(8,128)(2,1)S(1)} %get-tuple-element.689), channel_id=1, source_target_pairs={{0,16},{16,32},{32,48},{48,64},{64,80},{80,96},{96,112},{112,128},... | collective-permute-start | bytes 245768 | tf_op jit(solution)/shard_map/while/body/eval_jaxpr/ppermute | solution.py:16
  450.1 481.9 %while.34 = (s32[]{:T(128)}, bf16[16,2560]{1,0:T(8,128)(2,1)S(1)}, bf16[8,16,2560]{2,1,0:T(8,128)(2,1)S(1)}, bf16[8,16,2560]{2,1,0:T(8,128)(2,1)S(1)}, s32[23]{0...) while((s32[]{:T(128)}, bf16[16,2560]{1,0:T(8,128)(2,1)S(1)}, ...), condition=%wide.region_7.8_spmd, body=%wide.region_4.7_spmd.sunk | while | flops 210780160 | bytes 14503326 | solution.py:132
  464.2 10.3 collective-permute-done.1
  488.6 12.8 %collective-permute-done.1 = bf16[16,2560]{1,0:T(8,128)(2,1)S(1)} collective-permute-done((bf16[16,2560]{1,0:T(8,128)(2,1)S(1)}, bf16[16,2560]{1,0:T(8,128)(2,1)S(1)}, u32[]{:S(2)}, u32[]{:S(2)}) %collective-permute-start.1) | collective-permute-done | bytes 81952 | tf_op jit(solution)/shard_map/while/body/eval_jaxpr/ppermute | solution.py:16
  538.2 11.3 collective-permute-done.1
  575.5 132.8 %collective-permute-done.1 = bf16[16,2560]{1,0:T(8,128)(2,1)S(1)} collective-permute-done((bf16[16,2560]{1,0:T(8,128)(2,1)S(1)}, bf16[16,2560]{1,0:T(8,128)(2,1)S(1)}, u32[]{:S(2)}, u32[]{:S(2)}) %collective-permute-start.1) | collective-permute-done | bytes 81952 | tf_op jit(solution)/shard_map/while/body/eval_jaxpr/ppermute | solution.py:16
  709.6 11.7 %conditional.9 = (bf16[16,2560]{1,0:T(8,128)(2,1)S(1)}, bf16[8,16,2560]{2,1,0:T(8,128)(2,1)S(1)}, bf16[8,16,2560]{2,1,0:T(8,128)(2,1)S(1)}) conditional(s32[]{:T(128)} %convert_element_type.113, (bf16[8,16,2560]{2,1,0:T(8,128)(2,1)S(1)}, bf16[8,16,2560]{2,1,0:T(8,128)(2,1)S(1)}) %tuple.111, (pred[]{:T(512)}, s32[]{:T(128)}, s32[8]{0:T(128)S(1)}, ...), branch_computations={%region_5.5_spmd, %region_6.6_spmd} | conditional | flops 210780160 | bytes 14175335 | solution.py:126
  731.1 11.7 %conditional.9 = (bf16[16,2560]{1,0:T(8,128)(2,1)S(1)}, bf16[8,16,2560]{2,1,0:T(8,128)(2,1)S(1)}, bf16[8,16,2560]{2,1,0:T(8,128)(2,1)S(1)}) conditional(s32[]{:T(128)} %convert_element_type.113, (bf16[8,16,2560]{2,1,0:T(8,128)(2,1)S(1)}, bf16[8,16,2560]{2,1,0:T(8,128)(2,1)S(1)}) %tuple.111, (pred[]{:T(512)}, s32[]{:T(128)}, s32[8]{0:T(128)S(1)}, ...), branch_computations={%region_5.5_spmd, %region_6.6_spmd} | conditional | flops 210780160 | bytes 14175335 | solution.py:126
  752.5 11.7 %conditional.9 = (bf16[16,2560]{1,0:T(8,128)(2,1)S(1)}, bf16[8,16,2560]{2,1,0:T(8,128)(2,1)S(1)}, bf16[8,16,2560]{2,1,0:T(8,128)(2,1)S(1)}) conditional(s32[]{:T(128)} %convert_element_type.113, (bf16[8,16,2560]{2,1,0:T(8,128)(2,1)S(1)}, bf16[8,16,2560]{2,1,0:T(8,128)(2,1)S(1)}) %tuple.111, (pred[]{:T(512)}, s32[]{:T(128)}, s32[8]{0:T(128)S(1)}, ...), branch_computations={%region_5.5_spmd, %region_6.6_spmd} | conditional | flops 210780160 | bytes 14175335 | solution.py:126
  773.9 11.7 %conditional.9 = (bf16[16,2560]{1,0:T(8,128)(2,1)S(1)}, bf16[8,16,2560]{2,1,0:T(8,128)(2,1)S(1)}, bf16[8,16,2560]{2,1,0:T(8,128)(2,1)S(1)}) conditional(s32[]{:T(128)} %convert_element_type.113, (bf16[8,16,2560]{2,1,0:T(8,128)(2,1)S(1)}, bf16[8,16,2560]{2,1,0:T(8,128)(2,1)S(1)}) %tuple.111, (pred[]{:T(512)}, s32[]{:T(128)}, s32[8]{0:T(128)S(1)}, ...), branch_computations={%region_5.5_spmd, %region_6.6_spmd} | conditional | flops 210780160 | bytes 14175335 | solution.py:126
  795.3 11.7 %conditional.9 = (bf16[16,2560]{1,0:T(8,128)(2,1)S(1)}, bf16[8,16,2560]{2,1,0:T(8,128)(2,1)S(1)}, bf16[8,16,2560]{2,1,0:T(8,128)(2,1)S(1)}) conditional(s32[]{:T(128)} %convert_element_type.113, (bf16[8,16,2560]{2,1,0:T(8,128)(2,1)S(1)}, bf16[8,16,2560]{2,1,0:T(8,128)(2,1)S(1)}) %tuple.111, (pred[]{:T(512)}, s32[]{:T(128)}, s32[8]{0:T(128)S(1)}, ...), branch_computations={%region_5.5_spmd, %region_6.6_spmd} | conditional | flops 210780160 | bytes 14175335 | solution.py:126
  816.8 11.7 %conditional.9 = (bf16[16,2560]{1,0:T(8,128)(2,1)S(1)}, bf16[8,16,2560]{2,1,0:T(8,128)(2,1)S(1)}, bf16[8,16,2560]{2,1,0:T(8,128)(2,1)S(1)}) conditional(s32[]{:T(128)} %convert_element_type.113, (bf16[8,16,2560]{2,1,0:T(8,128)(2,1)S(1)}, bf16[8,16,2560]{2,1,0:T(8,128)(2,1)S(1)}) %tuple.111, (pred[]{:T(512)}, s32[]{:T(128)}, s32[8]{0:T(128)S(1)}, ...), branch_computations={%region_5.5_spmd, %region_6.6_spmd} | conditional | flops 210780160 | bytes 14175335 | solution.py:126
  838.7 11.7 %conditional.9 = (bf16[16,2560]{1,0:T(8,128)(2,1)S(1)}, bf16[8,16,2560]{2,1,0:T(8,128)(2,1)S(1)}, bf16[8,16,2560]{2,1,0:T(8,128)(2,1)S(1)}) conditional(s32[]{:T(128)} %convert_element_type.113, (bf16[8,16,2560]{2,1,0:T(8,128)(2,1)S(1)}, bf16[8,16,2560]{2,1,0:T(8,128)(2,1)S(1)}) %tuple.111, (pred[]{:T(512)}, s32[]{:T(128)}, s32[8]{0:T(128)S(1)}, ...), branch_computations={%region_5.5_spmd, %region_6.6_spmd} | conditional | flops 210780160 | bytes 14175335 | solution.py:126
  859.6 11.7 %conditional.9 = (bf16[16,2560]{1,0:T(8,128)(2,1)S(1)}, bf16[8,16,2560]{2,1,0:T(8,128)(2,1)S(1)}, bf16[8,16,2560]{2,1,0:T(8,128)(2,1)S(1)}) conditional(s32[]{:T(128)} %convert_element_type.113, (bf16[8,16,2560]{2,1,0:T(8,128)(2,1)S(1)}, bf16[8,16,2560]{2,1,0:T(8,128)(2,1)S(1)}) %tuple.111, (pred[]{:T(512)}, s32[]{:T(128)}, s32[8]{0:T(128)S(1)}, ...), branch_computations={%region_5.5_spmd, %region_6.6_spmd} | conditional | flops 210780160 | bytes 14175335 | solution.py:126
  879.0 16.3 %collective-permute-start.1 = (bf16[16,2560]{1,0:T(8,128)(2,1)S(1)}, bf16[16,2560]{1,0:T(8,128)(2,1)S(1)}, u32[]{:S(2)}, u32[]{:S(2)}) collective-permute-start(bf16[16,2560]{1,0:T(8,128)(2,1)S(1)} %get-tuple-element.704), channel_id=1, source_target_pairs={{16,0},{32,16},{48,32},{64,48},{80,64},{96,80},{112,96},{128,112},... | collective-permute-start | bytes 245768 | tf_op jit(solution)/shard_map/while/body/eval_jaxpr/ppermute | solution.py:16
  908.3 11.9 %collective-permute-start.1 = (bf16[16,2560]{1,0:T(8,128)(2,1)S(1)}, bf16[16,2560]{1,0:T(8,128)(2,1)S(1)}, u32[]{:S(2)}, u32[]{:S(2)}) collective-permute-start(bf16[16,2560]{1,0:T(8,128)(2,1)S(1)} %get-tuple-element.704), channel_id=1, source_target_pairs={{16,0},{32,16},{48,32},{64,48},{80,64},{96,80},{112,96},{128,112},... | collective-permute-start | bytes 245768 | tf_op jit(solution)/shard_map/while/body/eval_jaxpr/ppermute | solution.py:16
  935.1 125.0 %all-reduce.2.cloned.1.call-done = bf16[640,640]{1,0:T(8,128)(2,1)} async-done(((bf16[640,640]{1,0:T(8,128)(2,1)}), bf16[640,640]{1,0:T(8,128)(2,1)}) %all-reduce.2.cloned.1.call-update) | async-done | bytes 819216 | tf_op jit(solution)/shard_map/psum | solution.py:164
  1064.9 17.5 %collective-permute-done.2 = bf16[640,640]{1,0:T(8,128)(2,1)} collective-permute-done((bf16[640,640]{1,0:T(8,128)(2,1)S(1)}, bf16[640,640]{1,0:T(8,128)(2,1)}, u32[]{:S(2)}, u32[]{:S(2)}) %collective-permute-start.2) | collective-permute-done | bytes 819232 | tf_op jit(solution)/shard_map/ppermute | solution.py:22
  1083.7 36.5 %conditional.4 = (bf16[640,640]{1,0:T(8,128)(2,1)S(1)}) conditional(s32[]{:T(128)} %convert_element_type.73, () %tuple.78, f32[640,640]{1,0:T(8,128)S(1)} %convert_element_type.78), branch_computations={%region_9.10_spmd, %region_10.13_spmd} | conditional | flops 18880512000 | bytes 27038756 | solution.py:173
  1120.3 30.1 %conditional.5 = (f32[640,640]{1,0:T(8,128)S(1)}) conditional(s32[]{:T(128)} %convert_element_type.81, f32[640,640]{1,0:T(8,128)S(1)} %get-tuple-element.553, () %tuple.79), branch_computations={%region_13.16_spmd, %region_16.17_spmd} | conditional | flops 18880512000 | bytes 27857956 | solution.py:172
  (302 shorter events, 676.7 us)
Async XLA Ops:
  7.2 83.7 %all-gather.3.cloned.1.call-start = ((), (), s32[]{:S(2)}) async-start(), calls=%async_computation.1 | async-start | bytes 13926400 | tf_op jit(solution)/shard_map/all_gather | solution.py:62
  7.9 1052.3 %all-reduce.2.cloned.1.call-start = ((), (), s32[]{:S(2)}) async-start(), calls=%async_computation | async-start | bytes 1638400 | tf_op jit(solution)/shard_map/psum | solution.py:164
  121.8 37.0 %collective-permute-start = (bf16[16,2560]{1,0:T(8,128)(2,1)S(1)}, bf16[16,2560]{1,0:T(8,128)(2,1)S(1)}, u32[]{:S(2)}, u32[]{:S(2)}) collective-permute-start(bf16[16,2560]{1,0:T(8,128)(2,1)S(1)} %get-tuple-element.689), channel_id=1, source_target_pairs={{0,16},{16,32},{32,48},{48,64},{64,80},{80,96},{96,112},{112,128},... | collective-permute-start | bytes 245768 | tf_op jit(solution)/shard_map/while/body/eval_jaxpr/ppermute | solution.py:16
  319.5 12.0 %collective-permute-start = (bf16[16,2560]{1,0:T(8,128)(2,1)S(1)}, bf16[16,2560]{1,0:T(8,128)(2,1)S(1)}, u32[]{:S(2)}, u32[]{:S(2)}) collective-permute-start(bf16[16,2560]{1,0:T(8,128)(2,1)S(1)} %get-tuple-element.689), channel_id=1, source_target_pairs={{0,16},{16,32},{32,48},{48,64},{64,80},{80,96},{96,112},{112,128},... | collective-permute-start | bytes 245768 | tf_op jit(solution)/shard_map/while/body/eval_jaxpr/ppermute | solution.py:16
  342.5 12.0 %collective-permute-start = (bf16[16,2560]{1,0:T(8,128)(2,1)S(1)}, bf16[16,2560]{1,0:T(8,128)(2,1)S(1)}, u32[]{:S(2)}, u32[]{:S(2)}) collective-permute-start(bf16[16,2560]{1,0:T(8,128)(2,1)S(1)} %get-tuple-element.689), channel_id=1, source_target_pairs={{0,16},{16,32},{32,48},{48,64},{64,80},{80,96},{96,112},{112,128},... | collective-permute-start | bytes 245768 | tf_op jit(solution)/shard_map/while/body/eval_jaxpr/ppermute | solution.py:16
  365.6 12.0 %collective-permute-start = (bf16[16,2560]{1,0:T(8,128)(2,1)S(1)}, bf16[16,2560]{1,0:T(8,128)(2,1)S(1)}, u32[]{:S(2)}, u32[]{:S(2)}) collective-permute-start(bf16[16,2560]{1,0:T(8,128)(2,1)S(1)} %get-tuple-element.689), channel_id=1, source_target_pairs={{0,16},{16,32},{32,48},{48,64},{64,80},{80,96},{96,112},{112,128},... | collective-permute-start | bytes 245768 | tf_op jit(solution)/shard_map/while/body/eval_jaxpr/ppermute | solution.py:16
  388.7 14.2 %collective-permute-start = (bf16[16,2560]{1,0:T(8,128)(2,1)S(1)}, bf16[16,2560]{1,0:T(8,128)(2,1)S(1)}, u32[]{:S(2)}, u32[]{:S(2)}) collective-permute-start(bf16[16,2560]{1,0:T(8,128)(2,1)S(1)} %get-tuple-element.689), channel_id=1, source_target_pairs={{0,16},{16,32},{32,48},{48,64},{64,80},{80,96},{96,112},{112,128},... | collective-permute-start | bytes 245768 | tf_op jit(solution)/shard_map/while/body/eval_jaxpr/ppermute | solution.py:16
  413.8 12.0 %collective-permute-start = (bf16[16,2560]{1,0:T(8,128)(2,1)S(1)}, bf16[16,2560]{1,0:T(8,128)(2,1)S(1)}, u32[]{:S(2)}, u32[]{:S(2)}) collective-permute-start(bf16[16,2560]{1,0:T(8,128)(2,1)S(1)} %get-tuple-element.689), channel_id=1, source_target_pairs={{0,16},{16,32},{32,48},{48,64},{64,80},{80,96},{96,112},{112,128},... | collective-permute-start | bytes 245768 | tf_op jit(solution)/shard_map/while/body/eval_jaxpr/ppermute | solution.py:16
  436.9 12.2 %collective-permute-start = (bf16[16,2560]{1,0:T(8,128)(2,1)S(1)}, bf16[16,2560]{1,0:T(8,128)(2,1)S(1)}, u32[]{:S(2)}, u32[]{:S(2)}) collective-permute-start(bf16[16,2560]{1,0:T(8,128)(2,1)S(1)} %get-tuple-element.689), channel_id=1, source_target_pairs={{0,16},{16,32},{32,48},{48,64},{64,80},{80,96},{96,112},{112,128},... | collective-permute-start | bytes 245768 | tf_op jit(solution)/shard_map/while/body/eval_jaxpr/ppermute | solution.py:16
  451.4 9.6 collective-permute-start.1
  462.2 12.2 %collective-permute-start.1 = (bf16[16,2560]{1,0:T(8,128)(2,1)S(1)}, bf16[16,2560]{1,0:T(8,128)(2,1)S(1)}, u32[]{:S(2)}, u32[]{:S(2)}) collective-permute-start(bf16[16,2560]{1,0:T(8,128)(2,1)S(1)} %get-tuple-element.704), channel_id=1, source_target_pairs={{16,0},{32,16},{48,32},{64,48},{80,64},{96,80},{112,96},{128,112},... | collective-permute-start | bytes 245768 | tf_op jit(solution)/shard_map/while/body/eval_jaxpr/ppermute | solution.py:16
  475.7 9.7 collective-permute-start.1
  486.7 14.7 %collective-permute-start.1 = (bf16[16,2560]{1,0:T(8,128)(2,1)S(1)}, bf16[16,2560]{1,0:T(8,128)(2,1)S(1)}, u32[]{:S(2)}, u32[]{:S(2)}) collective-permute-start(bf16[16,2560]{1,0:T(8,128)(2,1)S(1)} %get-tuple-element.704), channel_id=1, source_target_pairs={{16,0},{32,16},{48,32},{64,48},{80,64},{96,80},{112,96},{128,112},... | collective-permute-start | bytes 245768 | tf_op jit(solution)/shard_map/while/body/eval_jaxpr/ppermute | solution.py:16
  502.7 9.1 collective-permute-start.1
  513.1 11.8 %collective-permute-start.1 = (bf16[16,2560]{1,0:T(8,128)(2,1)S(1)}, bf16[16,2560]{1,0:T(8,128)(2,1)S(1)}, u32[]{:S(2)}, u32[]{:S(2)}) collective-permute-start(bf16[16,2560]{1,0:T(8,128)(2,1)S(1)} %get-tuple-element.704), channel_id=1, source_target_pairs={{16,0},{32,16},{48,32},{64,48},{80,64},{96,80},{112,96},{128,112},... | collective-permute-start | bytes 245768 | tf_op jit(solution)/shard_map/while/body/eval_jaxpr/ppermute | solution.py:16
  526.2 8.8 collective-permute-start.1
  536.3 13.2 %collective-permute-start.1 = (bf16[16,2560]{1,0:T(8,128)(2,1)S(1)}, bf16[16,2560]{1,0:T(8,128)(2,1)S(1)}, u32[]{:S(2)}, u32[]{:S(2)}) collective-permute-start(bf16[16,2560]{1,0:T(8,128)(2,1)S(1)} %get-tuple-element.704), channel_id=1, source_target_pairs={{16,0},{32,16},{48,32},{64,48},{80,64},{96,80},{112,96},{128,112},... | collective-permute-start | bytes 245768 | tf_op jit(solution)/shard_map/while/body/eval_jaxpr/ppermute | solution.py:16
  560.5 11.8 %collective-permute-start.1 = (bf16[16,2560]{1,0:T(8,128)(2,1)S(1)}, bf16[16,2560]{1,0:T(8,128)(2,1)S(1)}, u32[]{:S(2)}, u32[]{:S(2)}) collective-permute-start(bf16[16,2560]{1,0:T(8,128)(2,1)S(1)} %get-tuple-element.704), channel_id=1, source_target_pairs={{16,0},{32,16},{48,32},{64,48},{80,64},{96,80},{112,96},{128,112},... | collective-permute-start | bytes 245768 | tf_op jit(solution)/shard_map/while/body/eval_jaxpr/ppermute | solution.py:16
  573.6 134.8 %collective-permute-start.1 = (bf16[16,2560]{1,0:T(8,128)(2,1)S(1)}, bf16[16,2560]{1,0:T(8,128)(2,1)S(1)}, u32[]{:S(2)}, u32[]{:S(2)}) collective-permute-start(bf16[16,2560]{1,0:T(8,128)(2,1)S(1)} %get-tuple-element.704), channel_id=1, source_target_pairs={{16,0},{32,16},{48,32},{64,48},{80,64},{96,80},{112,96},{128,112},... | collective-permute-start | bytes 245768 | tf_op jit(solution)/shard_map/while/body/eval_jaxpr/ppermute | solution.py:16
  828.5 9.0 collective-permute-start.1
  879.0 18.3 %collective-permute-start.1 = (bf16[16,2560]{1,0:T(8,128)(2,1)S(1)}, bf16[16,2560]{1,0:T(8,128)(2,1)S(1)}, u32[]{:S(2)}, u32[]{:S(2)}) collective-permute-start(bf16[16,2560]{1,0:T(8,128)(2,1)S(1)} %get-tuple-element.704), channel_id=1, source_target_pairs={{16,0},{32,16},{48,32},{64,48},{80,64},{96,80},{112,96},{128,112},... | collective-permute-start | bytes 245768 | tf_op jit(solution)/shard_map/while/body/eval_jaxpr/ppermute | solution.py:16
  908.3 14.0 %collective-permute-start.1 = (bf16[16,2560]{1,0:T(8,128)(2,1)S(1)}, bf16[16,2560]{1,0:T(8,128)(2,1)S(1)}, u32[]{:S(2)}, u32[]{:S(2)}) collective-permute-start(bf16[16,2560]{1,0:T(8,128)(2,1)S(1)} %get-tuple-element.704), channel_id=1, source_target_pairs={{16,0},{32,16},{48,32},{64,48},{80,64},{96,80},{112,96},{128,112},... | collective-permute-start | bytes 245768 | tf_op jit(solution)/shard_map/while/body/eval_jaxpr/ppermute | solution.py:16
  1061.5 20.9 %collective-permute-start.2 = (bf16[640,640]{1,0:T(8,128)(2,1)S(1)}, bf16[640,640]{1,0:T(8,128)(2,1)}, u32[]{:S(2)}, u32[]{:S(2)}) collective-permute-start(bf16[640,640]{1,0:T(8,128)(2,1)S(1)} %get-tuple-element.552), channel_id=1, source_target_pairs={{0,128},{16,144},{32,160},{48,176},{64,192},{80,208},{96,224},{112... | collective-permute-start | bytes 2457608 | tf_op jit(solution)/shard_map/ppermute | solution.py:22
  1120.2 30.2 %collective-permute-start.3 = (bf16[40,640]{1,0:T(8,128)(2,1)S(1)}, bf16[40,640]{1,0:T(8,128)(2,1)S(1)}, u32[]{:S(2)}, u32[]{:S(2)}) collective-permute-start(bf16[40,640]{1,0:T(8,128)(2,1)S(1)} %dynamic-slice_convert_fusion), channel_id=1, source_target_pairs={{0,128},{16,144},{32,160},{48,176},{64,192},{80,208},{96,224},{112... | collective-permute-start | bytes 153608 | tf_op jit(solution)/shard_map/ppermute | solution.py:22
  (29 other events, 304.3 us)
Sparse Core Ops, SparseCore 0:
  9.8 80.9 all-gather.2
  934.6 125.5 all-reduce.1
where the time goes:
time: 1170 us; the launch traced here: 1160 us
  waiting for transfers between devices  633 us (54%)
  starting transfers between devices  194 us (17%)
  matrix products  175 us (15%)
  loops' own time  72.3 us (6%)
  local copies, waits for them, and re-layouts  40.5 us (3%)
  other arithmetic  22.8 us (2%)
  between operations  20.3 us (2%)
    ppermute x46, waiting for transfers between devices, from_behind(): lax.ppermute(value, axis, [(source, source + steps) for source in range(i...  414 us
    ppermute x46, starting transfers between devices, from_behind(): lax.ppermute(value, axis, [(source, source + steps) for source in range(i...  192 us
    psum x1, waiting for transfers between devices, shards(): lax.psum((scaled + placed).astype(jnp.bfloat16), 'dp').astype(jnp.float32)  125 us
    all_gather x1, waiting for transfers between devices, shards(): full_weight = lax.all_gather(weights[0], 'dp', axis=0, tiled=True)  76.3 us
    dot_general x8, matrix products, backward_compute(): lax.dot_general(delta_now, full_weight, (((1,), (1,)), ((), ())), preferr...  65.7 us
    dot_general x8, matrix products, forward_compute(): preact = jnp.dot(current, full_weight, preferred_element_type=jnp.float32)  52.5 us
    dot_general x6, matrix products, newton_schulz(): jnp.dot(matrix, approx, precision=lax.Precision.HIGHEST, preferred_elemen...  28.3 us
    dot_general x6, matrix products, newton_schulz(): jnp.dot(approx, 2.0 * identity - product, precision=lax.Precision.HIGHEST...  28.2 us
  transfers between devices with their start and end apart: 50, of which 49 were waited for; matrix products, arithmetic and copies ran while one was open for 3% of the time, Pallas kernels for 0%

commit v1 on v0

v1 whole, which is shorter than its diff:
```python
import functools

import jax
import jax.numpy as jnp
from jax import lax
from jax.experimental import pallas as pl
from jax.experimental.pallas import tpu as pltpu
from jax.sharding import PartitionSpec as P

RETAIN = 0.6
DAMPING = 0.1
TERMS = 8
CORES = 2
MESH = pl.DeviceIdType.MESH


def kernel(
    sections,
    replicas,
    pieces,
    plan_ref,
    order_ref,
    x_ref,
    ct_ref,
    w_ref,
    old_ref,
    out_ref,
    grad_ref,
    inv_ref,
    w,
    wt,
    x_in,
    g_in,
    slope,
    delta,
    feats,
    old_all,
    matrix,
    local_sem,
    ring_send,
    ring_recv,
    sib_sem,
    fwd_send,
    fwd_recv,
    bwd_send,
    bwd_recv,
    feat_send,
    feat_recv,
    old_sem,
):
    micro, rows, width = x_in.shape
    shard = w_ref.shape[1]
    half = shard // 2
    band, order_size = old_ref.shape[2], old_ref.shape[3]
    piece = width // pieces
    zs = replicas // CORES
    s = lax.axis_index("section")
    r = lax.axis_index("dp")
    z, core = r // CORES, r % CORES
    first, last = s == 0, s == sections - 1
    z_right, z_left = (z + 1) % zs, (z + zs - 1) % zs
    right, left = z_right * CORES + core, z_left * CORES + core
    sibling = z * CORES + (1 - core)
    up, down = jnp.minimum(s + 1, sections - 1), jnp.maximum(s - 1, 0)

    barrier = pltpu.get_barrier_semaphore()

    def greet(i, _):
        pl.semaphore_signal(
            barrier, inc=1, device_id={"dp": (r + i) % replicas}, device_id_type=MESH
        )
        return 0

    lax.fori_loop(1, replicas, greet, 0)

    @pl.when(jnp.logical_not(last))
    def _():
        pl.semaphore_signal(barrier, inc=1, device_id={"section": up}, device_id_type=MESH)

    @pl.when(jnp.logical_not(first))
    def _():
        pl.semaphore_signal(barrier, inc=1, device_id={"section": down}, device_id_type=MESH)

    peers = replicas - 1 + jnp.where(first, 0, 1) + jnp.where(last, 0, 1)
    pl.semaphore_wait(barrier, peers)

    def w_rows(at_z, which):
        start = (at_z * CORES + core) * shard + which * half
        return w.at[pl.ds(pl.multiple_of(start, 16), half)]

    def copy(src, dst, send, recv, **device):
        return pltpu.make_async_remote_copy(
            src_ref=src,
            dst_ref=dst,
            send_sem=send,
            recv_sem=recv,
            device_id=device,
            device_id_type=MESH,
        )

    own_w = pltpu.make_async_copy(
        w_ref.at[0], w.at[pl.ds(pl.multiple_of(r * shard, 16), shard)], local_sem
    )

    def to_sibling(at_z, which):
        rows_there = w_rows(at_z, which)
        copy(rows_there, rows_there, sib_sem.at[0], sib_sem.at[1], dp=sibling).start()

    def ring_send_of(way, k):
        hop, which = k // 2, (k + way) % 2
        dst = w_rows((z + zs - hop) % zs if way == 0 else (z + hop) % zs, which)
        src = w_ref.at[0, pl.ds(which * half, half)] if hop == 0 else dst
        there = right if way == 0 else left
        return copy(src, dst, ring_send.at[way, k], ring_recv.at[way, k], dp=there)

    def ring_arrival(way, k):
        hop, which = k // 2 + 1, (k + way) % 2
        at_z = (z + zs - hop) % zs if way == 0 else (z + hop) % zs
        here = w_rows(at_z, which)
        there = right if way == 0 else left
        copy(here, here, ring_send.at[way, k], ring_recv.at[way, k], dp=there).wait_recv()
        return at_z, which

    own_w.start()
    for k in range(zs - 1):
        for way in range(2):
            came = ring_arrival(way, k - 2) if k >= 2 else None
            ring_send_of(way, k).start()
            if came:
                to_sibling(*came)
        if k == 0:
            own_w.wait()
        if k == 1:
            to_sibling(z, 0)
            to_sibling(z, 1)
    for k in range(zs - 3, zs - 1):
        for way in range(2):
            to_sibling(*ring_arrival(way, k))
    for k in range(zs - 1):
        for way in range(2):
            ring_send_of(way, k).wait_send()
    all_sib = w.at[pl.ds(0, zs * shard)]
    sib_wait = copy(all_sib, all_sib, sib_sem.at[0], sib_sem.at[1], dp=sibling)
    sib_wait.wait_recv()
    sib_wait.wait_send()

    block = plan_ref[s, 0]
    filled = plan_ref[s, 2]
    old_all[r] = old_ref[0, block]

    def send_old(i, _):
        copy(
            old_all.at[r], old_all.at[r], old_sem.at[0], old_sem.at[1], dp=(r + i) % replicas
        ).start()
        return 0

    lax.fori_loop(1, replicas, send_old, 0)

    def turn_weights():
        tile = 2 * 128
        spots = lax.broadcasted_iota(jnp.int32, (tile, tile), 0)
        eye = (spots == lax.broadcasted_iota(jnp.int32, (tile, tile), 1)).astype(jnp.bfloat16)

        def turn(i, _):
            at = pl.ds(pl.multiple_of(i * tile, tile), tile)
            for j in range(pieces):
                cols = pl.ds(j * piece, piece)
                wt[cols, at] = lax.dot_general(
                    w[at, cols], eye, (((0,), (0,)), ((), ())), preferred_element_type=jnp.float32
                ).astype(jnp.bfloat16)
            return 0

        lax.fori_loop(0, width // tile, turn, 0)

    @pl.when(s >= sections // 2)
    def _():
        turn_weights()

    def forward(c, _):
        @pl.when(first)
        def _():
            x_in[c] = x_ref[order_ref[c]]

        @pl.when(jnp.logical_not(first))
        def _():
            copy(x_in.at[c], x_in.at[c], fwd_send.at[c], fwd_recv.at[c], section=up).wait_recv()

        x = x_in[c]
        for j in range(pieces):
            cols = pl.ds(j * piece, piece)
            pre = jnp.dot(x, w[:, cols], preferred_element_type=jnp.float32)
            gate = jax.nn.sigmoid(pre)
            out_ref[0, c, :, cols] = (
                x_in[c, :, cols].astype(jnp.float32) + pre * gate
            ).astype(jnp.bfloat16)

            @pl.when(jnp.logical_not(last))
            def _():
                copy(
                    out_ref.at[0, c, :, cols],
                    x_in.at[c, :, cols],
                    fwd_send.at[c],
                    fwd_recv.at[c],
                    section=up,
                ).start()

            slope[c, :, cols] = gate * (1.0 + pre * (1.0 - gate))
        return 0

    lax.fori_loop(0, micro, forward, 0)

    @pl.when(s < sections // 2)
    def _():
        turn_weights()

    place = block % (width // order_size)
    from_input = block < width // order_size

    def backward(c, _):
        @pl.when(last)
        def _():
            g_in[c] = ct_ref[order_ref[c]]

        @pl.when(jnp.logical_not(last))
        def _():
            copy(g_in.at[c], g_in.at[c], bwd_send.at[c], bwd_recv.at[c], section=down).wait_recv()

        delta[...] = (g_in[c].astype(jnp.float32) * slope[c]).astype(jnp.bfloat16)
        d = delta[...]
        for j in range(pieces):
            cols = pl.ds(j * piece, piece)
            back = jnp.dot(d, wt[:, cols], preferred_element_type=jnp.float32)
            grad_ref[0, c, :, cols] = (g_in[c, :, cols].astype(jnp.float32) + back).astype(
                jnp.bfloat16
            )

            @pl.when(jnp.logical_not(first))
            def _():
                copy(
                    grad_ref.at[0, c, :, cols],
                    g_in.at[c, :, cols],
                    bwd_send.at[c],
                    bwd_recv.at[c],
                    section=down,
                ).start()

        chosen = jnp.zeros((rows, order_size), jnp.bfloat16)
        for j in range(width // order_size):
            cols = pl.ds(j * order_size, order_size)
            here = jnp.where(from_input, x_in[c, :, cols], delta[:, cols])
            chosen = jnp.where(place == j, here, chosen)
        feats[c, r] = jnp.where(c < filled, chosen, jnp.zeros_like(chosen))

        def send_feats(i, _):
            copy(
                feats.at[c, r],
                feats.at[c, r],
                feat_send.at[c],
                feat_recv.at[c],
                dp=(r + i) % replicas,
            ).start()
            return 0

        lax.fori_loop(1, replicas, send_feats, 0)
        return 0

    lax.fori_loop(0, micro, backward, 0)

    matrix[...] = jnp.zeros_like(matrix)

    def gather_stats(c, _):
        others = feats.at[c, pl.ds(0, replicas - 1)]
        copy(others, others, feat_send.at[c], feat_recv.at[c], dp=sibling).wait_recv()
        v = feats[c].reshape(replicas * rows, order_size)
        matrix[...] += lax.dot_general(
            v, v, (((0,), (0,)), ((), ())), preferred_element_type=jnp.float32
        )
        return 0

    lax.fori_loop(0, micro, gather_stats, 0)
    others = old_all.at[pl.ds(0, replicas - 1)]
    old_wait = copy(others, others, old_sem.at[0], old_sem.at[1], dp=sibling)
    old_wait.wait_recv()
    scale = (1.0 - RETAIN) / (filled * (rows * replicas)).astype(jnp.float32)
    spots = lax.broadcasted_iota(jnp.int32, (order_size, order_size), 0)
    eye = spots == lax.broadcasted_iota(jnp.int32, (order_size, order_size), 1)
    full = (
        RETAIN * old_all[...].reshape(order_size, order_size)
        + scale * matrix[...]
        + jnp.where(eye, DAMPING, 0.0)
    )
    bound = jnp.max(jnp.sum(jnp.abs(full), axis=1, keepdims=True), axis=0, keepdims=True)
    unit = 1.0 / bound
    scaled = full * unit
    matrix[...] = scaled
    factor = scaled.astype(jnp.bfloat16)
    mine = lax.broadcasted_iota(jnp.int32, (band, order_size), 0) + r * band
    ones = (mine == lax.broadcasted_iota(jnp.int32, (band, order_size), 1)).astype(jnp.float32)
    total = 2.0 * ones - matrix[pl.ds(pl.multiple_of(r * band, 8), band), :]
    for _ in range(TERMS - 2):
        high = total.astype(jnp.bfloat16)
        low = (total - high.astype(jnp.float32)).astype(jnp.bfloat16)
        product = jnp.dot(high, factor, preferred_element_type=jnp.float32) + jnp.dot(
            low, factor, preferred_element_type=jnp.float32
        )
        total = ones + total - product
    inv_ref[0] = total * unit

    old_wait.wait_send()

    def drain(c, _):
        others = feats.at[c, pl.ds(0, replicas - 1)]
        copy(others, others, feat_send.at[c], feat_recv.at[c], dp=sibling).wait_send()

        @pl.when(jnp.logical_not(last))
        def _():
            copy(x_in.at[c], x_in.at[c], fwd_send.at[c], fwd_recv.at[c], section=up).wait_send()

        @pl.when(jnp.logical_not(first))
        def _():
            copy(g_in.at[c], g_in.at[c], bwd_send.at[c], bwd_recv.at[c], section=down).wait_send()

        return 0

    lax.fori_loop(0, micro, drain, 0)


def shards(sections, replicas, inputs, cotangent, weights, old_factor, plan, order):
    micro, rows, width = inputs.shape
    _, _, band, order_size = old_factor.shape
    pieces = 5 if width % 640 == 0 else width // 128
    vmem = pl.BlockSpec(memory_space=pltpu.VMEM)
    smem = pl.BlockSpec(memory_space=pltpu.SMEM)
    sems = pltpu.SemaphoreType.DMA
    zs = replicas // CORES
    return pl.pallas_call(
        functools.partial(kernel, sections, replicas, pieces),
        out_shape=(
            jax.ShapeDtypeStruct((1, micro, rows, width), jnp.bfloat16),
            jax.ShapeDtypeStruct((1, micro, rows, width), jnp.bfloat16),
            jax.ShapeDtypeStruct((1, band, order_size), jnp.float32),
        ),
        in_specs=[smem, smem, vmem, vmem, pl.BlockSpec(memory_space=pl.ANY), vmem],
        out_specs=(vmem, vmem, vmem),
        scratch_shapes=[
            pltpu.VMEM((width, width), jnp.bfloat16),
            pltpu.VMEM((width, width), jnp.bfloat16),
            pltpu.VMEM((micro, rows, width), jnp.bfloat16),
            pltpu.VMEM((micro, rows, width), jnp.bfloat16),
            pltpu.VMEM((micro, rows, width), jnp.float32),
            pltpu.VMEM((rows, width), jnp.bfloat16),
            pltpu.VMEM((micro, replicas, rows, order_size), jnp.bfloat16),
            pltpu.VMEM((replicas, band, order_size), jnp.float32),
            pltpu.VMEM((order_size, order_size), jnp.float32),
            sems,
            sems((2, zs - 1)),
            sems((2, zs - 1)),
            sems((2,)),
            sems((micro,)),
            sems((micro,)),
            sems((micro,)),
            sems((micro,)),
            sems((micro,)),
            sems((micro,)),
            sems((2,)),
        ],
        compiler_params=pltpu.CompilerParams(
            collective_id=0, has_side_effects=True, vmem_limit_bytes=56 * 2**20
        ),
    )(plan, order, inputs, cotangent, weights, old_factor)


def solution(mesh):
    return jax.shard_map(
        functools.partial(shards, mesh.shape["section"], mesh.shape["dp"]),
        mesh=mesh,
        in_specs=(
            P(None, "dp", None),
            P(None, "dp", None),
            P("section", "dp", None),
            P("section", None, "dp", None),
            P(),
            P(),
        ),
        out_specs=(
            P("section", None, "dp", None),
            P("section", None, "dp", None),
            P("section", "dp", None),
        ),
        check_vma=False,
    )
```

time: 1170 us -> 305 us (0.26)
  the two profiles are of different devices: /device:TPU:8 before, /device:TPU:1 now
where the time goes in v1:
time: 305 us
  Pallas kernels  300 us (98%)
  local copies, waits for them, and re-layouts  5 us (2%)
    pallas_call x1, Pallas kernels, shards(): pl.pallas_call(functools.partial(kernel, sections, replicas, pieces), out...  300 us

profile of v1, /device:TPU:1, one launch (start us, length us, event | category | flops | bytes accessed | tf_op | source)
XLA Modules:
  0.0 305.2 jit_solution(915809209347624235)
XLA Ops:
  0.6 1.4 copy.9.plan_ref
  2.0 299.5 %shard_map.85 = (bf16[1,8,16,2560]{3,2,1,0:T(8,128)(2,1)}, bf16[1,8,16,2560]{3,2,1,0:T(8,128)(2,1)}, f32[1,40,640]{2,1,0:T(8,128)}) custom-call(s32[16,3]{1,0:T(8,128)} %copy.9.plan_ref, s32[8]{0:T(128)} %order_ref.1, bf16[8,16,2560]{2,1,0:T(8,128)(2,1)} %x_ref.1, bf16[8,16,2560]{2,1,0:T(8,128)(2,1)} %ct_ref.1, bf16[1,160,2560]{2,1,0:T(8,128)(2,1)} %w_ref.1, ...), custom_call_target="tpu_custom_call" | custom-call | tf_op jit(solution)/shard_map/pallas_call | solution.py:336
  301.5 0.0 copy-start
  301.6 2.0 copy.13
  303.6 0.0 copy-done
  303.6 0.0 copy-start.1
  303.6 0.8 copy.14
  304.4 0.1 copy-done.1
  304.6 0.6 copy.15
Async XLA Ops:
  301.5 2.0 copy-start
  303.6 1.0 copy-start.1

commit v2 on v1

v2 whole, which is shorter than its diff:
```python
import functools

import jax
import jax.numpy as jnp
from jax import lax
from jax.experimental import pallas as pl
from jax.experimental.pallas import tpu as pltpu
from jax.sharding import PartitionSpec as P

RETAIN = 0.6
DAMPING = 0.1
TERMS = 8
CORES = 2
BAND = 16
MESH = pl.DeviceIdType.MESH


def kernel(
    sections,
    replicas,
    pieces,
    plan_ref,
    order_ref,
    x_ref,
    ct_ref,
    w_ref,
    old_ref,
    out_ref,
    grad_ref,
    inv_ref,
    w,
    wt,
    ends,
    x_in,
    g_in,
    out,
    grad,
    slope,
    delta,
    feats,
    old_own,
    old_all,
    matrix,
    lent,
    local_sem,
    store_sem,
    ring_send,
    ring_recv,
    sib_sem,
    lend_sem,
    relay_send,
    relay_recv,
    back_send,
    back_recv,
    fwd_send,
    fwd_recv,
    bwd_send,
    bwd_recv,
    feat_send,
    feat_recv,
    feat_pass,
    feat_got,
    old_sem,
    old_pass,
):
    micro, rows, width = x_in.shape
    shard = w_ref.shape[1]
    band, order_size = old_ref.shape[2], old_ref.shape[3]
    piece = width // pieces
    zs = replicas // CORES
    lent_rows = lent.shape[1]
    bands = lent_rows // BAND
    parts = (
        (0, shard - 2 * lent_rows),
        (shard - 2 * lent_rows, lent_rows),
        (shard - lent_rows, lent_rows),
    )
    group = max(1, sections // 4)
    s = lax.axis_index("section")
    r = lax.axis_index("dp")
    z, core = r // CORES, r % CORES
    first, last = s == 0, s == sections - 1
    borrows, lends = s < group, s >= sections - group
    partner = (s + sections - group) % sections
    partner = jnp.where(borrows, partner, jnp.where(lends, s - (sections - group), s))
    sibling = z * CORES + (1 - core)
    up, down = jnp.minimum(s + 1, sections - 1), jnp.maximum(s - 1, 0)

    def along_z(steps):
        return (z + steps) % zs

    def copy(src, dst, send, recv, **device):
        return pltpu.make_async_remote_copy(
            src_ref=src,
            dst_ref=dst,
            send_sem=send,
            recv_sem=recv,
            device_id=device,
            device_id_type=MESH,
        )

    own_w = pltpu.make_async_copy(
        w_ref.at[0], w.at[pl.ds(pl.multiple_of(r * shard, 16), shard)], local_sem.at[0]
    )
    own_w.start()
    load_old = pltpu.make_async_copy(old_ref.at[0], old_own, local_sem.at[1])
    load_old.start()
    load_x = pltpu.make_async_copy(x_ref, ends, local_sem.at[2])
    load_ct = pltpu.make_async_copy(ct_ref, ends, local_sem.at[2])

    @pl.when(first)
    def _():
        load_x.start()

    @pl.when(last)
    def _():
        load_ct.start()

    barrier = pltpu.get_barrier_semaphore()

    def greet(i, _):
        there = along_z(i) * CORES + core
        pl.semaphore_signal(barrier, inc=1, device_id={"dp": there}, device_id_type=MESH)
        return 0

    lax.fori_loop(1, zs, greet, 0)
    pl.semaphore_signal(barrier, inc=1, device_id={"dp": sibling}, device_id_type=MESH)
    helped = jnp.logical_or(borrows, lends)

    @pl.when(jnp.logical_not(last))
    def _():
        pl.semaphore_signal(barrier, inc=1, device_id={"section": up}, device_id_type=MESH)

    @pl.when(jnp.logical_not(first))
    def _():
        pl.semaphore_signal(barrier, inc=1, device_id={"section": down}, device_id_type=MESH)

    @pl.when(helped)
    def _():
        pl.semaphore_signal(barrier, inc=1, device_id={"section": partner}, device_id_type=MESH)

    peers = zs + jnp.where(first, 0, 1) + jnp.where(last, 0, 1) + jnp.where(helped, 1, 0)
    pl.semaphore_wait(barrier, peers)

    def w_rows(at_z, part):
        start = (at_z * CORES + core) * shard + parts[part][0]
        return w.at[pl.ds(pl.multiple_of(start, 16), parts[part][1])]

    def own_rows(part):
        return w_ref.at[0, pl.ds(*parts[part])]

    def to_sibling(rows_there):
        copy(rows_there, rows_there, sib_sem.at[0], sib_sem.at[1], dp=sibling).start()

    def next_z(way):
        return along_z(1 if way == 0 else zs - 1) * CORES + core

    def from_z(way, hop):
        return along_z(zs - hop if way == 0 else hop)

    def hops(way, part):
        return zs // 2 if (way == 0) == (part == 0) else zs // 2 - 1

    def ring_copy(way, hop, part):
        spot = hop * 3 + part
        dst = w_rows(from_z(way, hop), part)
        src = own_rows(part) if hop == 0 else dst
        return copy(src, dst, ring_send.at[way, spot], ring_recv.at[way, spot], dp=next_z(way))

    def ring_arrival(way, hop, part):
        spot = hop * 3 + part
        here = w_rows(from_z(way, hop + 1), part)
        copy(
            here, here, ring_send.at[way, spot], ring_recv.at[way, spot], dp=next_z(way)
        ).wait_recv()
        return here

    def lent_band(at_z, i):
        return lent.at[at_z, pl.ds(i * BAND, BAND)]

    def lend(i):
        start = parts[2][0] + i * BAND
        return copy(
            w_ref.at[0, pl.ds(start, BAND)],
            lent_band(z, i),
            lend_sem.at[0, i],
            lend_sem.at[1, i],
            section=partner,
        )

    def relay_copy(way, hop, i, at=0):
        here = lent_band(from_z(way, hop + at), i)
        return copy(
            here, here, relay_send.at[way, hop, i], relay_recv.at[way, hop, i], dp=next_z(way)
        )

    def give_back(way, hop, i):
        at_z = from_z(way, hop + 1)
        start = (at_z * CORES + core) * shard + parts[2][0] + i * BAND
        return copy(
            lent_band(at_z, i),
            w.at[pl.ds(pl.multiple_of(start, 16), BAND)],
            back_send.at[way, hop, i],
            back_recv.at[way, hop, i],
            section=partner,
        )

    def back_arrival(way, hop):
        for i in range(bands):
            give_back(way, hop, i).wait_recv()
        to_sibling(w_rows(from_z(way, hop + 1), 2))

    lent_hops = (zs // 2, zs // 2 - 1)

    def ring(some_parts, extra):
        for hop in range(zs // 2 + 1):
            for part in some_parts:
                for way in range(2):
                    came = None
                    if 0 < hop <= hops(way, part):
                        came = ring_arrival(way, hop - 1, part)
                    if hop < hops(way, part):
                        ring_copy(way, hop, part).start()
                    if came is not None:
                        to_sibling(came)
            if hop == 0:
                own_w.wait()
                to_sibling(w.at[pl.ds(pl.multiple_of(r * shard, 16), shard)])
            if hop >= 2:
                extra(hop - 2)
        extra(zs // 2 - 1)

    @pl.when(borrows)
    def _():
        for i in range(bands):
            lend(i).start()

        def extra(hop):
            for way in range(2):
                if hop < lent_hops[way]:
                    back_arrival(way, hop)

        ring((0, 1), extra)

    @pl.when(lends)
    def _():
        for hop in range(zs // 2 + 1):
            for i in range(bands):
                if hop == 0:
                    lend(i).wait_recv()
                for way in range(2):
                    came = 0 < hop <= lent_hops[way]
                    if came:
                        relay_copy(way, hop - 1, i, 1).wait_recv()
                    if hop < lent_hops[way]:
                        relay_copy(way, hop, i).start()
                    if came:
                        give_back(way, hop - 1, i).start()

    @pl.when(jnp.logical_not(borrows))
    def _():
        ring((0, 1, 2), lambda hop: None)

    load_old.wait()
    block = plan_ref[0, s]
    filled = plan_ref[2, s]
    old_all[z, core] = old_own[block]

    def send_old(i, _):
        here = old_all.at[z, core]
        copy(here, here, old_sem.at[0], old_sem.at[1], dp=along_z(i) * CORES + core).start()
        return 0

    lax.fori_loop(1, zs, send_old, 0)
    all_sib = w.at[pl.ds(0, zs * shard)]
    sib_wait = copy(all_sib, all_sib, sib_sem.at[0], sib_sem.at[1], dp=sibling)
    sib_wait.wait_recv()

    def turn_weights():
        tile = 2 * 128
        spots = lax.broadcasted_iota(jnp.int32, (tile, tile), 0)
        eye = (spots == lax.broadcasted_iota(jnp.int32, (tile, tile), 1)).astype(jnp.bfloat16)

        def turn(i, _):
            at = pl.ds(pl.multiple_of(i * tile, tile), tile)
            for j in range(pieces):
                cols = pl.ds(j * piece, piece)
                wt[cols, at] = lax.dot_general(
                    w[at, cols], eye, (((0,), (0,)), ((), ())), preferred_element_type=jnp.float32
                ).astype(jnp.bfloat16)
            return 0

        lax.fori_loop(0, width // tile, turn, 0)

    def store(ref, c, whole_ref, sem):
        return pltpu.make_async_copy(ref.at[c], whole_ref.at[0, c], sem)

    def forward(c, count, sends):
        for i in range(count):
            arrival = copy(
                x_in.at[c + i], x_in.at[c + i], fwd_send.at[c + i], fwd_recv.at[c + i], section=up
            )
            if sends:

                @pl.when(first)
                def _():
                    x_in[c + i] = ends[order_ref[c + i]]

                @pl.when(jnp.logical_not(first))
                def _():
                    arrival.wait_recv()

            else:
                arrival.wait_recv()

        these = pl.ds(c, count)
        x = x_in[these].reshape(count * rows, width)
        for j in range(pieces):
            cols = pl.ds(j * piece, piece)
            pre = jnp.dot(x, w[:, cols], preferred_element_type=jnp.float32)
            pre = pre.reshape(count, rows, piece)
            gate = jax.nn.sigmoid(pre)
            out[these, :, cols] = (x_in[these, :, cols].astype(jnp.float32) + pre * gate).astype(
                jnp.bfloat16
            )
            if sends:
                copy(
                    out.at[c, :, cols],
                    x_in.at[c, :, cols],
                    fwd_send.at[c],
                    fwd_recv.at[c],
                    section=up,
                ).start()
            slope[these, :, cols] = gate * (1.0 + pre * (1.0 - gate))
        for i in range(count):
            store(out, c + i, out_ref, store_sem.at[0, c + i]).start()

    def forward_step(c, _):
        forward(c, 1, True)
        return 0

    @pl.when(first)
    def _():
        load_x.wait()

    @pl.when(jnp.logical_not(last))
    def _():
        lax.fori_loop(0, micro, forward_step, 0)

    turn_weights()

    own_old = old_all.at[:, core]
    some_old = old_all.at[pl.ds(0, zs - 1), core]
    copy(some_old, some_old, old_sem.at[0], old_sem.at[1], dp=sibling).wait_recv()
    pass_old = copy(own_old, own_old, old_pass.at[0], old_pass.at[1], dp=sibling)
    pass_old.start()
    matrix[...] = jnp.zeros_like(matrix)
    place = block % (width // order_size)
    from_input = block < width // order_size

    def gradient_in(c):
        @pl.when(last)
        def _():
            g_in[c] = ends[order_ref[c]]

        @pl.when(jnp.logical_not(last))
        def _():
            copy(g_in.at[c], g_in.at[c], bwd_send.at[c], bwd_recv.at[c], section=down).wait_recv()

        delta[c] = (g_in[c].astype(jnp.float32) * slope[c]).astype(jnp.bfloat16)

    def share_features(c):
        chosen = jnp.zeros((rows, order_size), jnp.bfloat16)
        for j in range(width // order_size):
            cols = pl.ds(j * order_size, order_size)
            here = jnp.where(from_input, x_in[c, :, cols], delta[c, :, cols])
            chosen = jnp.where(place == j, here, chosen)
        feats[c, core, z] = jnp.where(c < filled, chosen, jnp.zeros_like(chosen))

        def send_feats(i, _):
            here = feats.at[c, core, z]
            there = along_z(i) * CORES + core
            copy(here, here, feat_send.at[c], feat_recv.at[c], dp=there).start()
            return 0

        lax.fori_loop(1, zs, send_feats, 0)

    def feats_in(c):
        some = feats.at[c, core, pl.ds(0, zs - 1)]
        return copy(some, some, feat_send.at[c], feat_recv.at[c], dp=sibling)

    def feats_pass(c):
        here = feats.at[c, core]
        return copy(here, here, feat_pass.at[c], feat_got.at[c], dp=sibling)

    def pass_features(c, _=0):
        feats_in(c).wait_recv()
        feats_pass(c).start()
        return 0

    def add_stats(c, _=0):
        feats_pass(c).wait_recv()
        v = feats[c].reshape(replicas * rows, order_size)
        matrix[...] += lax.dot_general(
            v, v, (((0,), (0,)), ((), ())), preferred_element_type=jnp.float32
        )
        return 0

    def backward(c, count):
        for i in range(count):
            gradient_in(c + i)
        these = pl.ds(c, count)
        d = delta[these].reshape(count * rows, width)
        for j in range(pieces):
            cols = pl.ds(j * piece, piece)
            back = jnp.dot(d, wt[:, cols], preferred_element_type=jnp.float32)
            back = back.reshape(count, rows, piece)
            grad[these, :, cols] = (g_in[these, :, cols].astype(jnp.float32) + back).astype(
                jnp.bfloat16
            )
            copy(
                grad.at[c, :, cols],
                g_in.at[c, :, cols],
                bwd_send.at[c],
                bwd_recv.at[c],
                section=down,
            ).start()
        for i in range(1, count):
            copy(
                grad.at[c + i], g_in.at[c + i], bwd_send.at[c + i], bwd_recv.at[c + i], section=down
            ).start()
        for i in range(count):
            share_features(c + i)
            store(grad, c + i, grad_ref, store_sem.at[1, c + i]).start()

    def backward_step(c, _):
        backward(c, 1)
        return 0

    @pl.when(jnp.logical_not(jnp.logical_or(first, last)))
    def _():
        lax.fori_loop(0, micro, backward_step, 0)

    @pl.when(last)
    def _():
        load_ct.wait()

        def turn_round(c, count):
            forward(c, count, False)
            backward(c, count)

        def by_twos(i, _):
            turn_round(1 + 2 * i, 2)
            return 0

        turn_round(0, 1)
        lax.fori_loop(0, (micro - 2) // 2, by_twos, 0)
        turn_round(micro - 1, 1)

    @pl.when(jnp.logical_not(first))
    def _():
        lax.fori_loop(0, micro, pass_features, 0)
        lax.fori_loop(0, micro, add_stats, 0)

    lag = min(3, micro - 1)

    def backward_first(c, _):
        gradient_in(c)
        share_features(c)

        @pl.when(c >= lag)
        def _():
            pass_features(c - lag)

        @pl.when(c > lag)
        def _():
            add_stats(c - lag - 1)

        return 0

    @pl.when(first)
    def _():
        lax.fori_loop(0, micro, backward_first, 0)
        lax.fori_loop(micro - lag, micro - 1, pass_features, 0)
        add_stats(micro - lag - 1)

        def all_gradients(j, _):
            cols = pl.ds(pl.multiple_of(j * piece, 128), piece)
            d = delta[...].reshape(micro * rows, width)
            back = jnp.dot(d, wt[:, cols], preferred_element_type=jnp.float32)
            total = g_in[:, :, cols].astype(jnp.float32) + back.reshape(micro, rows, piece)
            grad[:, :, cols] = total.astype(jnp.bfloat16)
            return 0

        lax.fori_loop(0, pieces, all_gradients, 0)

        def store_all(c, _):
            store(grad, c, grad_ref, store_sem.at[1, c]).start()
            return 0

        lax.fori_loop(0, micro, store_all, 0)
        lax.fori_loop(micro - lag, micro - 1, add_stats, 0)
        pass_features(micro - 1)
        add_stats(micro - 1)

    pass_old.wait_recv()
    scale = (1.0 - RETAIN) / (filled * (rows * replicas)).astype(jnp.float32)
    spots = lax.broadcasted_iota(jnp.int32, (order_size, order_size), 0)
    eye = spots == lax.broadcasted_iota(jnp.int32, (order_size, order_size), 1)
    full = (
        RETAIN * old_all[...].reshape(order_size, order_size)
        + scale * matrix[...]
        + jnp.where(eye, DAMPING, 0.0)
    )
    bound = jnp.max(jnp.sum(jnp.abs(full), axis=1, keepdims=True), axis=0, keepdims=True)
    unit = 1.0 / bound
    scaled = full * unit
    matrix[...] = scaled
    factor = scaled.astype(jnp.bfloat16)
    row_ids = lax.broadcasted_iota(jnp.int32, (band, order_size), 0) + r * band
    ones = (row_ids == lax.broadcasted_iota(jnp.int32, (band, order_size), 1)).astype(jnp.float32)
    total = 2.0 * ones - matrix[pl.ds(pl.multiple_of(r * band, 8), band), :]
    for _ in range(TERMS - 2):
        high = total.astype(jnp.bfloat16)
        low = (total - high.astype(jnp.float32)).astype(jnp.bfloat16)
        product = jnp.dot(high, factor, preferred_element_type=jnp.float32) + jnp.dot(
            low, factor, preferred_element_type=jnp.float32
        )
        total = ones + total - product
    inv_ref[0] = total * unit

    def drain_ring(some_parts):
        for part in some_parts:
            for way in range(2):
                for hop in range(hops(way, part)):
                    ring_copy(way, hop, part).wait_send()

    drain_ring((0, 1))

    @pl.when(borrows)
    def _():
        for i in range(bands):
            lend(i).wait_send()

    @pl.when(jnp.logical_not(borrows))
    def _():
        drain_ring((2,))

    @pl.when(lends)
    def _():
        for way in range(2):
            for hop in range(lent_hops[way]):
                for i in range(bands):
                    relay_copy(way, hop, i).wait_send()
                    give_back(way, hop, i).wait_send()

    sib_wait.wait_send()
    copy(some_old, some_old, old_sem.at[0], old_sem.at[1], dp=sibling).wait_send()
    pass_old.wait_send()

    def drain(c, _):
        feats_in(c).wait_send()
        feats_pass(c).wait_send()
        store(out, c, out_ref, store_sem.at[0, c]).wait()
        store(grad, c, grad_ref, store_sem.at[1, c]).wait()

        @pl.when(jnp.logical_not(last))
        def _():
            copy(out.at[c], x_in.at[c], fwd_send.at[c], fwd_recv.at[c], section=up).wait_send()

        @pl.when(jnp.logical_not(first))
        def _():
            copy(grad.at[c], g_in.at[c], bwd_send.at[c], bwd_recv.at[c], section=down).wait_send()

        return 0

    lax.fori_loop(0, micro, drain, 0)


def shards(sections, replicas, inputs, cotangent, weights, old_factor, plan, order):
    micro, rows, width = inputs.shape
    _, blocks, band, order_size = old_factor.shape
    shard = weights.shape[1]
    lent_rows = shard // 16 * 3 // 10 * 16
    pieces = 5 if width % 640 == 0 else width // 128
    vmem = pl.BlockSpec(memory_space=pltpu.VMEM)
    smem = pl.BlockSpec(memory_space=pltpu.SMEM)
    free = pl.BlockSpec(memory_space=pl.ANY)
    hbm = pl.BlockSpec(memory_space=pltpu.HBM)
    sems = pltpu.SemaphoreType.DMA
    zs = replicas // CORES
    acts = pltpu.VMEM((micro, rows, width), jnp.bfloat16)
    return pl.pallas_call(
        functools.partial(kernel, sections, replicas, pieces),
        out_shape=(
            jax.ShapeDtypeStruct((1, micro, rows, width), jnp.bfloat16),
            jax.ShapeDtypeStruct((1, micro, rows, width), jnp.bfloat16),
            jax.ShapeDtypeStruct((1, band, order_size), jnp.float32),
        ),
        in_specs=[smem, smem, hbm, hbm, hbm, hbm],
        out_specs=(free, free, vmem),
        scratch_shapes=[
            pltpu.VMEM((width, width), jnp.bfloat16),
            pltpu.VMEM((width, width), jnp.bfloat16),
            acts,
            acts,
            acts,
            acts,
            acts,
            pltpu.VMEM((micro, rows, width), jnp.float32),
            acts,
            pltpu.VMEM((micro, CORES, zs, rows, order_size), jnp.bfloat16),
            pltpu.VMEM((blocks, band, order_size), jnp.float32),
            pltpu.VMEM((zs, CORES, band, order_size), jnp.float32),
            pltpu.VMEM((order_size, order_size), jnp.float32),
            pltpu.VMEM((zs, lent_rows, width), jnp.bfloat16),
            sems((3,)),
            sems((2, micro)),
            sems((2, 3 * (zs // 2))),
            sems((2, 3 * (zs // 2))),
            sems((2,)),
            sems((2, lent_rows // BAND)),
            sems((2, zs // 2, lent_rows // BAND)),
            sems((2, zs // 2, lent_rows // BAND)),
            sems((2, zs // 2, lent_rows // BAND)),
            sems((2, zs // 2, lent_rows // BAND)),
            sems((micro,)),
            sems((micro,)),
            sems((micro,)),
            sems((micro,)),
            sems((micro,)),
            sems((micro,)),
            sems((micro,)),
            sems((micro,)),
            sems((2,)),
            sems((2,)),
        ],
        compiler_params=pltpu.CompilerParams(
            collective_id=0, has_side_effects=True, vmem_limit_bytes=52 * 2**20
        ),
    )(plan.T, order, inputs, cotangent, weights, old_factor)


def solution(mesh):
    return jax.shard_map(
        functools.partial(shards, mesh.shape["section"], mesh.shape["dp"]),
        mesh=mesh,
        in_specs=(
            P(None, "dp", None),
            P(None, "dp", None),
            P("section", "dp", None),
            P("section", None, "dp", None),
            P(),
            P(),
        ),
        out_specs=(
            P("section", None, "dp", None),
            P("section", None, "dp", None),
            P("section", "dp", None),
        ),
        check_vma=False,
    )
```

time: 305 us -> 270 us (0.89)
  Pallas kernels: 300 us -> 266 us
    pallas_call x1, Pallas kernels: 300 us -> 266 us  [shards(): pl.pallas_call(functools.partial(kernel, sections, replicas, pieces), out...]
where the time goes in v2:
time: 270 us
  Pallas kernels  266 us (99%)
  local copies, waits for them, and re-layouts  3.65 us (1%)
    pallas_call x1, Pallas kernels, shards(): pl.pallas_call(functools.partial(kernel, sections, replicas, pieces), out...  266 us

profile of v2, /device:TPU:1, one launch (start us, length us, event | category | flops | bytes accessed | tf_op | source)
XLA Modules:
  0.0 270.4 jit_solution(3130675682064253488)
XLA Ops:
  0.6 0.0 copy-start.1
  0.6 0.6 copy-done.1
  1.3 0.0 copy-start
  1.3 0.7 copy-done
  2.0 266.1 %shard_map.85 = (bf16[1,8,16,2560]{3,2,1,0:T(8,128)(2,1)S(1)}, bf16[1,8,16,2560]{3,2,1,0:T(8,128)(2,1)S(1)}, f32[1,40,640]{2,1,0:T(8,128)S(1)}) custom-call(s32[3,16]{1,0:T(4,128)S(1)} %bitcast.1, s32[8]{0:T(128)S(1)} %copy-done.1, bf16[8,16,2560]{2,1,0:T(8,128)(2,1)} %x_ref.1, bf16[8,16,2560]{2,1,0:T(8,128)(2,1)} %ct_ref.1, bf16[1,160,2560]{2,1,0:T(8,128)(2,1)} %w_ref.1, ...), custom_call_target="tpu_custom_call" | custom-call | tf_op jit(solution)/shard_map/pallas_call | solution.py:593
  268.0 0.8 copy.12
  268.9 0.8 copy.13
  269.7 0.6 copy.14
Async XLA Ops:
  0.6 0.7 copy-start.1
  1.3 0.7 copy-start

commit v3 on v2

--- a/solution.py
+++ b/solution.py
@@ -295,6 +295,16 @@
     def store(ref, c, whole_ref, sem):
         return pltpu.make_async_copy(ref.at[c], whole_ref.at[0, c], sem)
 
+    def by_pieces(value, matrix_ref, finish):
+        before = None
+        for j in range(pieces):
+            cols = pl.ds(j * piece, piece)
+            product = jnp.dot(value, matrix_ref[:, cols], preferred_element_type=jnp.float32)
+            if before is not None:
+                finish(*before)
+            before = (cols, product)
+        finish(*before)
+
     def forward(c, count, sends):
         for i in range(count):
             arrival = copy(
@@ -315,9 +325,8 @@
 
         these = pl.ds(c, count)
         x = x_in[these].reshape(count * rows, width)
-        for j in range(pieces):
-            cols = pl.ds(j * piece, piece)
-            pre = jnp.dot(x, w[:, cols], preferred_element_type=jnp.float32)
+
+        def finish(cols, pre):
             pre = pre.reshape(count, rows, piece)
             gate = jax.nn.sigmoid(pre)
             out[these, :, cols] = (x_in[these, :, cols].astype(jnp.float32) + pre * gate).astype(
@@ -332,6 +341,8 @@
                     section=up,
                 ).start()
             slope[these, :, cols] = gate * (1.0 + pre * (1.0 - gate))
+
+        by_pieces(x, w, finish)
         for i in range(count):
             store(out, c + i, out_ref, store_sem.at[0, c + i]).start()
 
@@ -343,18 +354,30 @@
     def _():
         load_x.wait()
 
+    @pl.when(s >= sections // 2)
+    def _():
+        turn_weights()
+
     @pl.when(jnp.logical_not(last))
     def _():
         lax.fori_loop(0, micro, forward_step, 0)
 
-    turn_weights()
+    @pl.when(s < sections // 2)
+    def _():
+        turn_weights()
 
     own_old = old_all.at[:, core]
     some_old = old_all.at[pl.ds(0, zs - 1), core]
     copy(some_old, some_old, old_sem.at[0], old_sem.at[1], dp=sibling).wait_recv()
     pass_old = copy(own_old, own_old, old_pass.at[0], old_pass.at[1], dp=sibling)
     pass_old.start()
-    matrix[...] = jnp.zeros_like(matrix)
+    pass_old.wait_recv()
+    scale = (1.0 - RETAIN) / (filled * (rows * replicas)).astype(jnp.float32)
+    spots = lax.broadcasted_iota(jnp.int32, (order_size, order_size), 0)
+    eye = spots == lax.broadcasted_iota(jnp.int32, (order_size, order_size), 1)
+    matrix[...] = RETAIN * old_all[...].reshape(order_size, order_size) + jnp.where(
+        eye, DAMPING, 0.0
+    )
     place = block % (width // order_size)
     from_input = block < width // order_size
 
@@ -377,13 +400,10 @@
             chosen = jnp.where(place == j, here, chosen)
         feats[c, core, z] = jnp.where(c < filled, chosen, jnp.zeros_like(chosen))
 
-        def send_feats(i, _):
+        for i in sorted(range(1, zs), key=lambda i: -min(i, zs - i)):
             here = feats.at[c, core, z]
             there = along_z(i) * CORES + core
             copy(here, here, feat_send.at[c], feat_recv.at[c], dp=there).start()
-            return 0
-
-        lax.fori_loop(1, zs, send_feats, 0)
 
     def feats_in(c):
         some = feats.at[c, core, pl.ds(0, zs - 1)]
@@ -401,7 +421,7 @@
     def add_stats(c, _=0):
         feats_pass(c).wait_recv()
         v = feats[c].reshape(replicas * rows, order_size)
-        matrix[...] += lax.dot_general(
+        matrix[...] += scale * lax.dot_general(
             v, v, (((0,), (0,)), ((), ())), preferred_element_type=jnp.float32
         )
         return 0
@@ -411,9 +431,8 @@
             gradient_in(c + i)
         these = pl.ds(c, count)
         d = delta[these].reshape(count * rows, width)
-        for j in range(pieces):
-            cols = pl.ds(j * piece, piece)
-            back = jnp.dot(d, wt[:, cols], preferred_element_type=jnp.float32)
+
+        def finish(cols, back):
             back = back.reshape(count, rows, piece)
             grad[these, :, cols] = (g_in[these, :, cols].astype(jnp.float32) + back).astype(
                 jnp.bfloat16
@@ -425,6 +444,8 @@
                 bwd_recv.at[c],
                 section=down,
             ).start()
+
+        by_pieces(d, wt, finish)
         for i in range(1, count):
             copy(
                 grad.at[c + i], g_in.at[c + i], bwd_send.at[c + i], bwd_recv.at[c + i], section=down
@@ -503,28 +524,16 @@
         pass_features(micro - 1)
         add_stats(micro - 1)
 
-    pass_old.wait_recv()
-    scale = (1.0 - RETAIN) / (filled * (rows * replicas)).astype(jnp.float32)
-    spots = lax.broadcasted_iota(jnp.int32, (order_size, order_size), 0)
-    eye = spots == lax.broadcasted_iota(jnp.int32, (order_size, order_size), 1)
-    full = (
-        RETAIN * old_all[...].reshape(order_size, order_size)
-        + scale * matrix[...]
-        + jnp.where(eye, DAMPING, 0.0)
-    )
+    full = matrix[...]
     bound = jnp.max(jnp.sum(jnp.abs(full), axis=1, keepdims=True), axis=0, keepdims=True)
     unit = 1.0 / bound
-    scaled = full * unit
-    matrix[...] = scaled
-    factor = scaled.astype(jnp.bfloat16)
+    factor = (full * unit).astype(jnp.bfloat16)
     row_ids = lax.broadcasted_iota(jnp.int32, (band, order_size), 0) + r * band
     ones = (row_ids == lax.broadcasted_iota(jnp.int32, (band, order_size), 1)).astype(jnp.float32)
-    total = 2.0 * ones - matrix[pl.ds(pl.multiple_of(r * band, 8), band), :]
+    total = 2.0 * ones - matrix[pl.ds(pl.multiple_of(r * band, 8), band), :] * unit
     for _ in range(TERMS - 2):
-        high = total.astype(jnp.bfloat16)
-        low = (total - high.astype(jnp.float32)).astype(jnp.bfloat16)
-        product = jnp.dot(high, factor, preferred_element_type=jnp.float32) + jnp.dot(
-            low, factor, preferred_element_type=jnp.float32
+        product = jnp.dot(
+            total.astype(jnp.bfloat16), factor, preferred_element_type=jnp.float32
         )
         total = ones + total - product
     inv_ref[0] = total * unit

time: 270 us -> 255 us (0.944)
  Pallas kernels: 266 us -> 250 us
    pallas_call x1, Pallas kernels: 266 us -> 250 us  [shards(): pl.pallas_call(functools.partial(kernel, sections, replicas, pieces), out...]
where the time goes in v3:
time: 255 us
  Pallas kernels  250 us (98%)
  local copies, waits for them, and re-layouts  3.65 us (1%)
    pallas_call x1, Pallas kernels, shards(): pl.pallas_call(functools.partial(kernel, sections, replicas, pieces), out...  250 us

profile of v3, /device:TPU:1, one launch (start us, length us, event | category | flops | bytes accessed | tf_op | source)
XLA Modules:
  0.0 254.5 jit_solution(4464779649390521726)
XLA Ops:
  0.6 0.0 copy-start.1
  0.6 0.6 copy-done.1
  1.3 0.0 copy-start
  1.3 0.7 copy-done
  2.0 250.2 %shard_map.85 = (bf16[1,8,16,2560]{3,2,1,0:T(8,128)(2,1)S(1)}, bf16[1,8,16,2560]{3,2,1,0:T(8,128)(2,1)S(1)}, f32[1,40,640]{2,1,0:T(8,128)S(1)}) custom-call(s32[3,16]{1,0:T(4,128)S(1)} %bitcast.1, s32[8]{0:T(128)S(1)} %copy-done.1, bf16[8,16,2560]{2,1,0:T(8,128)(2,1)} %x_ref.1, bf16[8,16,2560]{2,1,0:T(8,128)(2,1)} %ct_ref.1, bf16[1,160,2560]{2,1,0:T(8,128)(2,1)} %w_ref.1, ...), custom_call_target="tpu_custom_call" | custom-call | tf_op jit(solution)/shard_map/pallas_call | solution.py:602
  252.2 0.8 copy.12
  253.0 0.8 copy.13
  253.9 0.6 copy.14
Async XLA Ops:
  0.6 0.7 copy-start.1
  1.3 0.7 copy-start

commit v4 on v3

--- a/solution.py
+++ b/solution.py
@@ -67,6 +67,9 @@
     shard = w_ref.shape[1]
     band, order_size = old_ref.shape[2], old_ref.shape[3]
     piece = width // pieces
+    unit = piece // 2
+    sizes = [3 * unit] + [piece] * (pieces - 2) + [unit]
+    cuts = [pl.ds(sum(sizes[:j]), sizes[j]) for j in range(pieces)]
     zs = replicas // CORES
     lent_rows = lent.shape[1]
     bands = lent_rows // BAND
@@ -297,12 +300,11 @@
 
     def by_pieces(value, matrix_ref, finish):
         before = None
-        for j in range(pieces):
-            cols = pl.ds(j * piece, piece)
+        for j, cols in enumerate(cuts):
             product = jnp.dot(value, matrix_ref[:, cols], preferred_element_type=jnp.float32)
             if before is not None:
                 finish(*before)
-            before = (cols, product)
+            before = (j, cols, product)
         finish(*before)
 
     def forward(c, count, sends):
@@ -326,8 +328,8 @@
         these = pl.ds(c, count)
         x = x_in[these].reshape(count * rows, width)
 
-        def finish(cols, pre):
-            pre = pre.reshape(count, rows, piece)
+        def finish(_, cols, pre):
+            pre = pre.reshape(count, rows, cols.size)
             gate = jax.nn.sigmoid(pre)
             out[these, :, cols] = (x_in[these, :, cols].astype(jnp.float32) + pre * gate).astype(
                 jnp.bfloat16
@@ -392,7 +394,7 @@
 
         delta[c] = (g_in[c].astype(jnp.float32) * slope[c]).astype(jnp.bfloat16)
 
-    def share_features(c):
+    def choose_features(c):
         chosen = jnp.zeros((rows, order_size), jnp.bfloat16)
         for j in range(width // order_size):
             cols = pl.ds(j * order_size, order_size)
@@ -400,10 +402,18 @@
             chosen = jnp.where(place == j, here, chosen)
         feats[c, core, z] = jnp.where(c < filled, chosen, jnp.zeros_like(chosen))
 
+
+    def feature_copies(c):
+        copies = []
         for i in sorted(range(1, zs), key=lambda i: -min(i, zs - i)):
             here = feats.at[c, core, z]
             there = along_z(i) * CORES + core
-            copy(here, here, feat_send.at[c], feat_recv.at[c], dp=there).start()
+            copies.append(copy(here, here, feat_send.at[c], feat_recv.at[c], dp=there))
+        return copies
+
+    def share_features(c):
+        for each in feature_copies(c):
+            each.start()
 
     def feats_in(c):
         some = feats.at[c, core, pl.ds(0, zs - 1)]
@@ -426,14 +436,15 @@
         )
         return 0
 
-    def backward(c, count):
+    def backward(c, count, chosen_before):
+        leaving = [each for b in chosen_before for each in feature_copies(b)]
         for i in range(count):
             gradient_in(c + i)
         these = pl.ds(c, count)
         d = delta[these].reshape(count * rows, width)
 
-        def finish(cols, back):
-            back = back.reshape(count, rows, piece)
+        def finish(j, cols, back):
+            back = back.reshape(count, rows, cols.size)
             grad[these, :, cols] = (g_in[these, :, cols].astype(jnp.float32) + back).astype(
                 jnp.bfloat16
             )
@@ -444,6 +455,8 @@
                 bwd_recv.at[c],
                 section=down,
             ).start()
+            for each in leaving[j::pieces]:
+                each.start()
 
         by_pieces(d, wt, finish)
         for i in range(1, count):
@@ -451,32 +464,43 @@
                 grad.at[c + i], g_in.at[c + i], bwd_send.at[c + i], bwd_recv.at[c + i], section=down
             ).start()
         for i in range(count):
-            share_features(c + i)
+            choose_features(c + i)
             store(grad, c + i, grad_ref, store_sem.at[1, c + i]).start()
 
     def backward_step(c, _):
-        backward(c, 1)
-        return 0
-
-    @pl.when(jnp.logical_not(jnp.logical_or(first, last)))
-    def _():
-        lax.fori_loop(0, micro, backward_step, 0)
-
-    @pl.when(last)
-    def _():
-        load_ct.wait()
-
-        def turn_round(c, count):
-            forward(c, count, False)
-            backward(c, count)
+        backward(c, 1, [c - 1])
+        return 0
+
+    near_last = jnp.logical_and(s >= sections - 2, jnp.logical_not(first))
+
+    @pl.when(jnp.logical_not(jnp.logical_or(first, near_last)))
+    def _():
+        backward(0, 1, [])
+        lax.fori_loop(1, micro, backward_step, 0)
+        share_features(micro - 1)
+
+    @pl.when(near_last)
+    def _():
+        @pl.when(last)
+        def _():
+            load_ct.wait()
+
+        def turn_round(c, count, chosen_before):
+            @pl.when(last)
+            def _():
+                forward(c, count, False)
+
+            backward(c, count, chosen_before)
 
         def by_twos(i, _):
-            turn_round(1 + 2 * i, 2)
+            turn_round(1 + 2 * i, 2, [2 * i - 1, 2 * i])
             return 0
 
-        turn_round(0, 1)
-        lax.fori_loop(0, (micro - 2) // 2, by_twos, 0)
-        turn_round(micro - 1, 1)
+        turn_round(0, 1, [])
+        turn_round(1, 2, [0])
+        lax.fori_loop(1, (micro - 2) // 2, by_twos, 0)
+        turn_round(micro - 1, 1, [micro - 3, micro - 2])
+        share_features(micro - 1)
 
     @pl.when(jnp.logical_not(first))
     def _():
@@ -487,6 +511,7 @@
 
     def backward_first(c, _):
         gradient_in(c)
+        choose_features(c)
         share_features(c)
 
         @pl.when(c >= lag)
@@ -526,17 +551,17 @@
 
     full = matrix[...]
     bound = jnp.max(jnp.sum(jnp.abs(full), axis=1, keepdims=True), axis=0, keepdims=True)
-    unit = 1.0 / bound
-    factor = (full * unit).astype(jnp.bfloat16)
+    inverse_bound = 1.0 / bound
+    factor = (full * inverse_bound).astype(jnp.bfloat16)
     row_ids = lax.broadcasted_iota(jnp.int32, (band, order_size), 0) + r * band
     ones = (row_ids == lax.broadcasted_iota(jnp.int32, (band, order_size), 1)).astype(jnp.float32)
-    total = 2.0 * ones - matrix[pl.ds(pl.multiple_of(r * band, 8), band), :] * unit
+    total = 2.0 * ones - matrix[pl.ds(pl.multiple_of(r * band, 8), band), :] * inverse_bound
     for _ in range(TERMS - 2):
         product = jnp.dot(
             total.astype(jnp.bfloat16), factor, preferred_element_type=jnp.float32
         )
         total = ones + total - product
-    inv_ref[0] = total * unit
+    inv_ref[0] = total * inverse_bound
 
     def drain_ring(some_parts):
         for part in some_parts:

time: 255 us -> 255 us (level)
  no operation moved by 1% of the time
where the time goes in v4:
time: 255 us
  Pallas kernels  251 us (98%)
  local copies, waits for them, and re-layouts  3.65 us (1%)
    pallas_call x1, Pallas kernels, shards(): pl.pallas_call(functools.partial(kernel, sections, replicas, pieces), out...  251 us

profile of v4, /device:TPU:1, one launch (start us, length us, event | category | flops | bytes accessed | tf_op | source)
XLA Modules:
  0.0 254.9 jit_solution(10745336140996387931)
XLA Ops:
  0.6 0.0 copy-start.1
  0.6 0.6 copy-done.1
  1.3 0.0 copy-start
  1.3 0.7 copy-done
  2.0 250.6 %shard_map.85 = (bf16[1,8,16,2560]{3,2,1,0:T(8,128)(2,1)S(1)}, bf16[1,8,16,2560]{3,2,1,0:T(8,128)(2,1)S(1)}, f32[1,40,640]{2,1,0:T(8,128)S(1)}) custom-call(s32[3,16]{1,0:T(4,128)S(1)} %bitcast.1, s32[8]{0:T(128)S(1)} %copy-done.1, bf16[8,16,2560]{2,1,0:T(8,128)(2,1)} %x_ref.1, bf16[8,16,2560]{2,1,0:T(8,128)(2,1)} %ct_ref.1, bf16[1,160,2560]{2,1,0:T(8,128)(2,1)} %w_ref.1, ...), custom_call_target="tpu_custom_call" | custom-call | tf_op jit(solution)/shard_map/pallas_call | solution.py:627
  252.6 0.8 copy.12
  253.4 0.8 copy.13
  254.3 0.6 copy.14
Async XLA Ops:
  0.6 0.7 copy-start.1
  1.3 0.7 copy-start

commit v5 on v3

--- a/solution.py
+++ b/solution.py
@@ -458,16 +458,23 @@
         backward(c, 1)
         return 0
 
-    @pl.when(jnp.logical_not(jnp.logical_or(first, last)))
+    near_last = jnp.logical_and(s >= sections - 2, jnp.logical_not(first))
+
+    @pl.when(jnp.logical_not(jnp.logical_or(first, near_last)))
     def _():
         lax.fori_loop(0, micro, backward_step, 0)
 
-    @pl.when(last)
-    def _():
-        load_ct.wait()
+    @pl.when(near_last)
+    def _():
+        @pl.when(last)
+        def _():
+            load_ct.wait()
 
         def turn_round(c, count):
-            forward(c, count, False)
+            @pl.when(last)
+            def _():
+                forward(c, count, False)
+
             backward(c, count)
 
         def by_twos(i, _):

time: 255 us -> 254 us (level)
  no operation moved by 1% of the time
where the time goes in v5:
time: 254 us
  Pallas kernels  250 us (98%)
  local copies, waits for them, and re-layouts  3.65 us (1%)
    pallas_call x1, Pallas kernels, shards(): pl.pallas_call(functools.partial(kernel, sections, replicas, pieces), out...  250 us

profile of v5, /device:TPU:1, one launch (start us, length us, event | category | flops | bytes accessed | tf_op | source)
XLA Modules:
  0.0 254.2 jit_solution(8066109928617594852)
XLA Ops:
  0.6 0.0 copy-start.1
  0.6 0.6 copy-done.1
  1.3 0.0 copy-start
  1.3 0.7 copy-done
  2.0 249.9 %shard_map.85 = (bf16[1,8,16,2560]{3,2,1,0:T(8,128)(2,1)S(1)}, bf16[1,8,16,2560]{3,2,1,0:T(8,128)(2,1)S(1)}, f32[1,40,640]{2,1,0:T(8,128)S(1)}) custom-call(s32[3,16]{1,0:T(4,128)S(1)} %bitcast.1, s32[8]{0:T(128)S(1)} %copy-done.1, bf16[8,16,2560]{2,1,0:T(8,128)(2,1)} %x_ref.1, bf16[8,16,2560]{2,1,0:T(8,128)(2,1)} %ct_ref.1, bf16[1,160,2560]{2,1,0:T(8,128)(2,1)} %w_ref.1, ...), custom_call_target="tpu_custom_call" | custom-call | tf_op jit(solution)/shard_map/pallas_call | solution.py:609
  251.9 0.8 copy.12
  252.7 0.8 copy.13
  253.6 0.6 copy.14
Async XLA Ops:
  0.6 0.7 copy-start.1
  1.3 0.7 copy-start

commit v6 on v5

--- a/solution.py
+++ b/solution.py
@@ -392,7 +392,7 @@
 
         delta[c] = (g_in[c].astype(jnp.float32) * slope[c]).astype(jnp.bfloat16)
 
-    def share_features(c):
+    def choose_features(c):
         chosen = jnp.zeros((rows, order_size), jnp.bfloat16)
         for j in range(width // order_size):
             cols = pl.ds(j * order_size, order_size)
@@ -400,21 +400,51 @@
             chosen = jnp.where(place == j, here, chosen)
         feats[c, core, z] = jnp.where(c < filled, chosen, jnp.zeros_like(chosen))
 
-        for i in sorted(range(1, zs), key=lambda i: -min(i, zs - i)):
-            here = feats.at[c, core, z]
-            there = along_z(i) * CORES + core
-            copy(here, here, feat_send.at[c], feat_recv.at[c], dp=there).start()
-
-    def feats_in(c):
-        some = feats.at[c, core, pl.ds(0, zs - 1)]
-        return copy(some, some, feat_send.at[c], feat_recv.at[c], dp=sibling)
+
+    right, left = range(1, zs // 2 + 1), range(1, (zs - 1) // 2 + 1)
+    near = [d for d in right if d <= 2] + [-d for d in left if d <= 2]
+    far = [d for d in right if d > 2] + [-d for d in left if d > 2]
+
+    def send_feats(c, origin, steps, which):
+        here = feats.at[c, core, along_z(zs + origin)]
+        there = along_z(zs + steps) * CORES + core
+        copy(here, here, feat_send.at[which, c], feat_recv.at[which, c], dp=there).start()
+
+    def feats_in(c, which):
+        some = feats.at[c, core, pl.ds(0, len(far) if which else len(near))]
+        return copy(some, some, feat_send.at[which, c], feat_recv.at[which, c], dp=sibling)
+
+    def send_on(c):
+        feats_in(c, 0).wait_recv()
+        for d in far:
+            back = -2 if d > 0 else 2
+            send_feats(c, back, d + back, 1)
+
+    def share_features(c):
+        choose_features(c)
+        for d in near:
+            send_feats(c, 0, d, 0)
+
+        @pl.when(c == micro - 1)
+        def _():
+            for d in far:
+                send_feats(c, 0, d, 1)
+
+        @pl.when(c >= 2)
+        def _():
+            send_on(c - 2)
 
     def feats_pass(c):
         here = feats.at[c, core]
         return copy(here, here, feat_pass.at[c], feat_got.at[c], dp=sibling)
 
     def pass_features(c, _=0):
-        feats_in(c).wait_recv()
+        @pl.when(c == micro - 1)
+        def _():
+            feats_in(c, 0).wait_recv()
+
+        if far:
+            feats_in(c, 1).wait_recv()
         feats_pass(c).start()
         return 0
 
@@ -487,10 +517,11 @@
 
     @pl.when(jnp.logical_not(first))
     def _():
+        send_on(micro - 2)
         lax.fori_loop(0, micro, pass_features, 0)
         lax.fori_loop(0, micro, add_stats, 0)
 
-    lag = min(3, micro - 1)
+    lag = min(4, micro - 1)
 
     def backward_first(c, _):
         gradient_in(c)
@@ -509,8 +540,7 @@
     @pl.when(first)
     def _():
         lax.fori_loop(0, micro, backward_first, 0)
-        lax.fori_loop(micro - lag, micro - 1, pass_features, 0)
-        add_stats(micro - lag - 1)
+        send_on(micro - 2)
 
         def all_gradients(j, _):
             cols = pl.ds(pl.multiple_of(j * piece, 128), piece)
@@ -527,8 +557,12 @@
             return 0
 
         lax.fori_loop(0, micro, store_all, 0)
-        lax.fori_loop(micro - lag, micro - 1, add_stats, 0)
+        add_stats(micro - lag - 1)
+        lax.fori_loop(micro - lag, micro - 2, pass_features, 0)
+        lax.fori_loop(micro - lag, micro - 2, add_stats, 0)
+        pass_features(micro - 2)
         pass_features(micro - 1)
+        add_stats(micro - 2)
         add_stats(micro - 1)
 
     full = matrix[...]
@@ -575,7 +609,9 @@
     pass_old.wait_send()
 
     def drain(c, _):
-        feats_in(c).wait_send()
+        feats_in(c, 0).wait_send()
+        if far:
+            feats_in(c, 1).wait_send()
         feats_pass(c).wait_send()
         store(out, c, out_ref, store_sem.at[0, c]).wait()
         store(grad, c, grad_ref, store_sem.at[1, c]).wait()
@@ -644,8 +680,8 @@
             sems((micro,)),
             sems((micro,)),
             sems((micro,)),
-            sems((micro,)),
-            sems((micro,)),
+            sems((2, micro)),
+            sems((2, micro)),
             sems((micro,)),
             sems((micro,)),
             sems((2,)),

time: 254 us -> 251 us (0.988)
  Pallas kernels: 250 us -> 247 us
    pallas_call x1, Pallas kernels: 250 us -> 247 us  [shards(): pl.pallas_call(functools.partial(kernel, sections, replicas, pieces), out...]
where the time goes in v6:
time: 251 us
  Pallas kernels  247 us (98%)
  local copies, waits for them, and re-layouts  3.65 us (1%)
    pallas_call x1, Pallas kernels, shards(): pl.pallas_call(functools.partial(kernel, sections, replicas, pieces), out...  247 us

profile of v6, /device:TPU:1, one launch (start us, length us, event | category | flops | bytes accessed | tf_op | source)
XLA Modules:
  0.0 251.3 jit_solution(5874607788613243124)
XLA Ops:
  0.6 0.0 copy-start.1
  0.6 0.6 copy-done.1
  1.3 0.0 copy-start
  1.3 0.7 copy-done
  2.0 247.0 %shard_map.85 = (bf16[1,8,16,2560]{3,2,1,0:T(8,128)(2,1)S(1)}, bf16[1,8,16,2560]{3,2,1,0:T(8,128)(2,1)S(1)}, f32[1,40,640]{2,1,0:T(8,128)S(1)}) custom-call(s32[3,16]{1,0:T(4,128)S(1)} %bitcast.1, s32[8]{0:T(128)S(1)} %copy-done.1, bf16[8,16,2560]{2,1,0:T(8,128)(2,1)} %x_ref.1, bf16[8,16,2560]{2,1,0:T(8,128)(2,1)} %ct_ref.1, bf16[1,160,2560]{2,1,0:T(8,128)(2,1)} %w_ref.1, ...), custom_call_target="tpu_custom_call" | custom-call | tf_op jit(solution)/shard_map/pallas_call | solution.py:645
  249.0 0.8 copy.12
  249.8 0.8 copy.13
  250.6 0.6 copy.14
Async XLA Ops:
  0.6 0.7 copy-start.1
  1.3 0.7 copy-start

commit v7 on v6

--- a/solution.py
+++ b/solution.py
@@ -417,18 +417,19 @@
     def send_on(c):
         feats_in(c, 0).wait_recv()
         for d in far:
-            back = -2 if d > 0 else 2
-            send_feats(c, back, d + back, 1)
+            way = 1 - 2 * core if d == zs // 2 else (1 if d > 0 else -1)
+            send_feats(c, -2 * way, (abs(d) - 2) * way, 1)
 
     def share_features(c):
         choose_features(c)
-        for d in near:
+
+        @pl.when(c == micro - 1)
+        def _():
+            for d in sorted(far, key=abs, reverse=True):
+                send_feats(c, 0, d, 1)
+
+        for d in sorted(near, key=abs, reverse=True):
             send_feats(c, 0, d, 0)
-
-        @pl.when(c == micro - 1)
-        def _():
-            for d in far:
-                send_feats(c, 0, d, 1)
 
         @pl.when(c >= 2)
         def _():

time: 251 us -> 250 us (level)
  no operation moved by 1% of the time
where the time goes in v7:
time: 250 us
  Pallas kernels  245 us (98%)
  local copies, waits for them, and re-layouts  3.65 us (1%)
    pallas_call x1, Pallas kernels, shards(): pl.pallas_call(functools.partial(kernel, sections, replicas, pieces), out...  245 us

profile of v7, /device:TPU:1, one launch (start us, length us, event | category | flops | bytes accessed | tf_op | source)
XLA Modules:
  0.0 249.7 jit_solution(16178702760745634350)
XLA Ops:
  0.6 0.0 copy-start.1
  0.6 0.6 copy-done.1
  1.3 0.0 copy-start
  1.3 0.7 copy-done
  2.0 245.4 %shard_map.85 = (bf16[1,8,16,2560]{3,2,1,0:T(8,128)(2,1)S(1)}, bf16[1,8,16,2560]{3,2,1,0:T(8,128)(2,1)S(1)}, f32[1,40,640]{2,1,0:T(8,128)S(1)}) custom-call(s32[3,16]{1,0:T(4,128)S(1)} %bitcast.1, s32[8]{0:T(128)S(1)} %copy-done.1, bf16[8,16,2560]{2,1,0:T(8,128)(2,1)} %x_ref.1, bf16[8,16,2560]{2,1,0:T(8,128)(2,1)} %ct_ref.1, bf16[1,160,2560]{2,1,0:T(8,128)(2,1)} %w_ref.1, ...), custom_call_target="tpu_custom_call" | custom-call | tf_op jit(solution)/shard_map/pallas_call | solution.py:646
  247.4 0.8 copy.12
  248.2 0.8 copy.13
  249.1 0.6 copy.14
Async XLA Ops:
  0.6 0.7 copy-start.1
  1.3 0.7 copy-start
